TPU v7x, 512 devices: a whole 4x8x8 slice. The times are simulated.
512 devices in a mesh: dp: 8 (over x, core), roll: 16 (over z, y_hi), tp: 4 (over y_lo).
Axes of the slice: x: 4, y: 8 (y_hi: 2, y_lo: 4; y = y_hi * 4 + y_lo), z: 8, core: 2. Of those that a mesh axis runs over, the one named last changes fastest.
Arguments:
- input_gradient_pieces: float32 [8, 2, 64, 12288], P('dp', None, ('roll', 'tp')), may hold values from -6 to 6
- output_gradient_pieces: float32 [8, 2, 64, 14336], P('dp', None, 'tp', 'roll'), may hold values from -6 to 6
- adapter_input_factor: float32 [2, 64, 12288], P(None, ('roll', 'tp'), 'dp'), may hold values from -4 to 4
- input_factor_mean: float32 [2, 64, 12288], P(None, ('roll', 'tp'), 'dp'), may hold values from -6 to 6
- input_factor_variance: float32 [2, 64, 12288], P(None, ('roll', 'tp'), 'dp'), may hold values from 0.1 to 1
- adapter_output_factor: float32 [2, 64, 14336], P(None, ('tp', 'dp'), 'roll'), may hold values from -4 to 4
- output_factor_mean: float32 [2, 64, 14336], P(None, ('tp', 'dp'), 'roll'), may hold values from -6 to 6
- output_factor_variance: float32 [2, 64, 14336], P(None, ('tp', 'dp'), 'roll'), may hold values from 0.1 to 1
- fixed_weight_codes: bfloat16 [2, 12288, 14336], P(None, ('dp', 'tp'), 'roll'), may hold values from -1 to 1
- fixed_block_scales: float32 [2, 96, 112], P(None, ('dp', 'tp'), 'roll'), may hold values from 0.25 to 1
Outputs:
- merged_codes: bfloat16 [2, 12288, 14336], P(None, ('dp', 'tp'), 'roll')
- merged_scales: float32 [2, 96, 112], P(None, ('dp', 'tp'), 'roll')
- updated_input_factor: float32 [2, 64, 12288], P(None, ('roll', 'tp'), 'dp')
- updated_input_mean: float32 [2, 64, 12288], P(None, ('roll', 'tp'), 'dp')
- updated_input_variance: float32 [2, 64, 12288], P(None, ('roll', 'tp'), 'dp')
- updated_output_factor: float32 [2, 64, 14336], P(None, ('tp', 'dp'), 'roll')
- updated_output_mean: float32 [2, 64, 14336], P(None, ('tp', 'dp'), 'roll')
- updated_output_variance: float32 [2, 64, 14336], P(None, ('tp', 'dp'), 'roll')
All inputs are finite; a program needn't handle non-finite values. Where the computation divides by a largest or mean magnitude, that divisor is 1e-20 or more.
Results may differ from a plain program's by a relative error of at most 0.007.
Values may be sent and summed in bfloat16 or wider, within the bound.
No kernel may reach another device: no remote copies, remote signals or barrier semaphores. Data moves between devices by JAX's collectives and lax.ppermute only.
A program may use at most 64 MiB of HBM per device.

v0:
```python
import jax
import jax.numpy as jnp
from jax import lax
from jax.sharding import PartitionSpec as P

QBLK = 128
STEP = 100


adapter_scale = 0.5
learn_rate = 0.05


def adaptive_moment_update(param, gradient, first, second):
    first_new = 0.9 * first + 0.1 * gradient
    second_new = 0.999 * second + 0.001 * gradient * gradient
    corr_one = 1.0 - 0.9**STEP
    corr_two = 1.0 - 0.999**STEP
    param_new = param - learn_rate * (first_new / corr_one) / (
        jnp.sqrt(second_new / corr_two) + 1e-08
    )
    return (param_new, first_new, second_new)


def requantize(frozen, scales, adapter_product):
    layer_count, row_count, col_count = frozen.shape
    block_extent = (layer_count, row_count // QBLK, QBLK, col_count // QBLK, QBLK)
    combined_weight = frozen.reshape(block_extent).astype(jnp.float32) * scales[:, :, None, :, None]
    combined_weight = combined_weight + adapter_scale * adapter_product.reshape(block_extent)
    block_peak = jnp.max(jnp.abs(combined_weight), axis=(2, 4)) + 1e-06
    requantized = (
        (combined_weight / block_peak[:, :, None, :, None])
        .astype(jnp.bfloat16)
        .reshape(frozen.shape)
    )
    return (requantized, block_peak)


def shards(
    input_gradient_pieces,
    output_gradient_pieces,
    adapter_input_factor,
    input_factor_mean,
    input_factor_variance,
    adapter_output_factor,
    output_factor_mean,
    output_factor_variance,
    fixed_weight_codes,
    fixed_block_scales,
):
    input_factor_gradient, output_factor_gradient = (
        lax.psum_scatter(
            input_gradient_pieces[0].astype(jnp.bfloat16), "dp", scatter_dimension=2, tiled=True
        ).astype(jnp.float32),
        lax.psum_scatter(
            output_gradient_pieces[0].astype(jnp.bfloat16), "dp", scatter_dimension=1, tiled=True
        ).astype(jnp.float32),
    )
    updated_input_factor, updated_input_mean, updated_input_variance = adaptive_moment_update(
        adapter_input_factor, input_factor_gradient, input_factor_mean, input_factor_variance
    )
    updated_output_factor, updated_output_mean, updated_output_variance = adaptive_moment_update(
        adapter_output_factor, output_factor_gradient, output_factor_mean, output_factor_variance
    )
    layer_count, tile_rows, tile_cols = fixed_weight_codes.shape
    sent_a = updated_input_factor.astype(jnp.bfloat16)
    sent_b = updated_output_factor.astype(jnp.bfloat16)
    whole_block = lax.all_gather(sent_a, ("roll", "tp"), axis=1, tiled=True)
    shard_index = lax.axis_index("tp")
    input_rows = lax.dynamic_slice_in_dim(whole_block, shard_index * tile_rows, tile_rows, 2)
    tensor_ranks = lax.all_gather(sent_b, "dp", axis=1, tiled=True)
    adapter_product = jnp.einsum(
        "lrw,lrc->lwc",
        input_rows,
        lax.all_gather(tensor_ranks, "tp", axis=1, tiled=True),
        preferred_element_type=jnp.float32,
    )
    merged_codes, merged_scales = requantize(
        fixed_weight_codes, fixed_block_scales, adapter_product
    )
    return (
        merged_codes,
        merged_scales,
        updated_input_factor,
        updated_input_mean,
        updated_input_variance,
        updated_output_factor,
        updated_output_mean,
        updated_output_variance,
    )


def solution(mesh):
    in_specs = (
        P("dp", None, ("roll", "tp"), None),
        P("dp", None, "tp", "roll"),
        P(None, ("roll", "tp"), "dp"),
        P(None, ("roll", "tp"), "dp"),
        P(None, ("roll", "tp"), "dp"),
        P(None, ("tp", "dp"), "roll"),
        P(None, ("tp", "dp"), "roll"),
        P(None, ("tp", "dp"), "roll"),
        P(None, ("dp", "tp"), "roll"),
        P(None, ("dp", "tp"), "roll"),
    )
    out_specs = (
        P(None, ("dp", "tp"), "roll"),
        P(None, ("dp", "tp"), "roll"),
        P(None, ("roll", "tp"), "dp"),
        P(None, ("roll", "tp"), "dp"),
        P(None, ("roll", "tp"), "dp"),
        P(None, ("tp", "dp"), "roll"),
        P(None, ("tp", "dp"), "roll"),
        P(None, ("tp", "dp"), "roll"),
    )
    return jax.shard_map(shards, mesh=mesh, in_specs=in_specs, out_specs=out_specs, check_vma=False)
```

profile of v0, /device:TPU:16, one launch (start us, length us, event | category | flops | bytes accessed | tf_op | source)
XLA Modules:
  0.0 188.4 jit_solution(15132214271874570472)
XLA Ops:
  7.2 0.0 reduce-scatter.5.cloned.1.call-start
  7.2 1.0 convert_bitcast_fusion
  8.2 10.0 %copy.31 = bf16[2,1,12288]{1,0,2:T(2,128)(2,1)} copy(bf16[2,1,12288]{2,1,0:T(2,128)(2,1)S(1)} %convert_bitcast_fusion) | data formatting | bytes 98304
  18.2 23.7 %bitcast_reduce_fusion = bf16[12288,2]{1,0:T(8,128)(2,1)} fusion(bf16[2,1,12288]{1,0,2:T(2,128)(2,1)} %copy.31), kind=kLoop, calls=%fused_computation | loop fusion | bytes 98304
  41.9 0.0 copy-start.1
  41.9 0.0 copy-start.2
  41.9 0.0 copy-start.3
  41.9 0.0 copy-start.4
  41.9 0.0 copy-start.8
  41.9 0.0 copy-start
  41.9 0.0 reduce-scatter.5.cloned.1.call-update
  42.0 0.8 copy-done.1
  42.8 26.1 %all-reduce = bf16[2,16,896]{2,1,0:T(8,128)(2,1)S(1)} all-reduce(bf16[2,16,896]{2,1,0:T(8,128)(2,1)S(1)} %convert_bitcast_fusion.1), channel_id=3, replica_groups=mesh['dp'=8,'roll'=16,'tp'=4] {'dp'}, use_global_device_ids=true, to_apply=%region_1.0.clone | all-reduce | flops 28672 | bytes 114688
  68.9 1.3 dynamic-slice
  70.8 0.0 copy-done.2
  70.9 0.0 copy-done.3
  70.9 0.0 copy-done.4
  70.9 0.7 fusion.6
  71.5 12.8 %all_gather.10 = bf16[2,16,896]{2,0,1:T(2,128)(2,1)S(1)} all-gather(bf16[2,2,896]{2,0,1:T(2,128)(2,1)S(1)} %copy.28), channel_id=1, replica_groups=mesh['dp'=8,'roll'=16,'tp'=4] {'dp'}, dimensions={1}, use_global_device_ids=true | all-gather | bytes 64512 | tf_op jit(solution)/shard_map/all_gather | solution.py:71
  84.3 0.0 copy-done.8
  84.3 0.0 copy-done
  84.3 2.6 %reshape.43 = f32[2,3,128,7,128]{4,3,2,1,0:T(8,128)} reshape(bf16[2,384,896]{2,1,0:T(8,128)(2,1)S(1)} %copy-done) | data formatting | bytes 4128768 | tf_op jit(solution)/shard_map/convert_element_type | solution.py:28
  87.0 0.3 mul.92
  87.3 0.0 copy-start.5
  87.3 0.0 copy-start.6
  87.3 0.0 copy-start.7
  87.3 1.8 mul.93
  89.1 15.6 %all_gather.11 = bf16[2,64,896]{2,1,0:T(8,128)(2,1)S(1)} all-gather(bf16[2,16,896]{2,1,0:T(8,128)(2,1)S(1)} %copy.29), channel_id=1, replica_groups=mesh['dp'=8,'roll'=16,'tp'=4] {'tp'}, dimensions={1}, use_global_device_ids=true | all-gather | bytes 286720 | tf_op jit(solution)/shard_map/all_gather | solution.py:75
  104.7 0.0 reduce-scatter.5.cloned.1.call-done
  104.7 3.2 %reshape_bitcast_fusion = bf16[2,1,1536]{1,0,2:T(2,128)(2,1)S(1)} fusion(bf16[1536,2]{1,0:T(8,128)(2,1)} %reduce-scatter.5.cloned.1.call-done), kind=kLoop, calls=%fused_computation.4 | loop fusion | bytes 12288
  107.9 0.6 copy.32
  108.5 0.0 copy-done.5
  108.5 0.0 copy-done.6
  108.5 0.0 copy-done.7
  108.5 0.7 fusion.4
  109.2 54.8 %all_gather.9 = bf16[2,64,1536]{2,0,1:T(2,128)(2,1)S(1)} all-gather(bf16[2,1,1536]{2,0,1:T(2,128)(2,1)S(1)} %copy.26), channel_id=1, replica_groups=mesh['dp'=8,'roll'=16,'tp'=4] {'roll','tp'}, dimensions={1}, use_global_device_ids=true | all-gather | bytes 399360 | tf_op jit(solution)/shard_map/all_gather | solution.py:68
  164.0 0.1 constant_dynamic-slice_fusion
  164.1 0.6 convolution_multiply_fusion
  164.7 1.9 %mul.121 = f32[2,3,128,7,128]{4,3,2,1,0:T(8,128)} reshape(f32[2,384,896]{2,1,0:T(8,128)S(1)} %convolution_multiply_fusion) | data formatting | bytes 5505024 | tf_op jit(solution)/shard_map/mul | solution.py:29
  166.6 3.5 %abs_reduce_fusion = f32[2,3,7]{2,1,0:T(4,128)S(1)} fusion(f32[2,3,128,7,128]{4,3,2,1,0:T(8,128)} %mul.121, f32[2,3,128,7,128]{4,3,2,1,0:T(8,128)} %reshape.43, f32[2,3,7]{2,1,0:T(4,128)S(1)} %copy.24), kind=kLoop, calls=%fused_computation.1 | loop fusion | flops 2752470 | bytes 5505360 | tf_op jit(solution)/shard_map/reduce_max | solution.py:30
  170.1 0.6 copy.30
  170.7 1.9 %div.39 = f32[2,3,128,7,128]{4,3,2,1,0:T(8,128)} broadcast(f32[2,3,7]{2,1,0:T(4,128)S(1)} %broadcast_add_fusion), dimensions={0,1,3} | broadcast | bytes 2752680 | tf_op jit(solution)/shard_map/div | solution.py:32
  172.6 4.4 %div.40 = f32[2,384,896]{2,1,0:T(8,128)} reshape(f32[2,3,128,7,128]{4,3,2,1,0:T(8,128)} %div.39) | data formatting | bytes 5505024 | tf_op jit(solution)/shard_map/div | solution.py:32
  177.0 4.6 %divide_convert_fusion = bf16[2,384,896]{2,1,0:T(8,128)(2,1)} fusion(f32[2,384,896]{2,1,0:T(8,128)} %div.40, f32[2,384,896]{2,1,0:T(8,128)S(1)} %convolution_multiply_fusion, f32[2,384,896]{2,1,0:T(8,128)} %mul.93, bf16[2,384,896]{2,1,0:T(8,128)(2,1)} %param.18), kind=kLoop, calls=%fused_computation.2 | loop fusion | flops 3440640 | bytes 11010048 | tf_op jit(solution)/shard_map/convert_element_type | solution.py:33
  (6 shorter events, 0.0 us)
Async XLA Ops:
  7.2 97.5 %reduce-scatter.5.cloned.1.call-start = ((), (), s32[]{:S(2)}) async-start(), calls=%async_computation.1 | async-start | bytes 3538944
  41.9 0.9 copy-start.1
  41.9 29.0 %copy-start.2 = (f32[2,2,896]{2,1,0:T(2,128)S(1)}, f32[2,2,896]{2,1,0:T(2,128)}, u32[]{:S(2)}) copy-start(f32[2,2,896]{2,1,0:T(2,128)} %param.15) | copy-start | bytes 43012
  41.9 29.0 %copy-start.3 = (f32[2,2,896]{2,1,0:T(2,128)S(1)}, f32[2,2,896]{2,1,0:T(2,128)}, u32[]{:S(2)}) copy-start(f32[2,2,896]{2,1,0:T(2,128)} %param.16) | copy-start | bytes 43012
  41.9 29.0 %copy-start.4 = (f32[2,2,896]{2,1,0:T(2,128)S(1)}, f32[2,2,896]{2,1,0:T(2,128)}, u32[]{:S(2)}) copy-start(f32[2,2,896]{2,1,0:T(2,128)} %param.17) | copy-start | bytes 43012
  41.9 42.4 %copy-start.8 = (f32[2,3,7]{2,0,1:T(2,128)S(1)}, f32[2,3,7]{2,0,1:T(2,128)}, u32[]{:S(2)}) copy-start(f32[2,3,7]{2,0,1:T(2,128)} %param.19) | copy-start | bytes 508
  41.9 42.4 %copy-start = (bf16[2,384,896]{2,1,0:T(8,128)(2,1)S(1)}, bf16[2,384,896]{2,1,0:T(8,128)(2,1)}, u32[]{:S(2)}) copy-start(bf16[2,384,896]{2,1,0:T(8,128)(2,1)} %param.18) | copy-start | bytes 4128772
  87.3 21.3 %copy-start.5 = (f32[2,1,1536]{2,1,0:T(1,128)S(1)}, f32[2,1,1536]{2,1,0:T(1,128)}, u32[]{:S(2)}) copy-start(f32[2,1,1536]{2,1,0:T(1,128)} %param.12) | copy-start | bytes 36868
  87.3 21.3 %copy-start.6 = (f32[2,1,1536]{2,1,0:T(1,128)S(1)}, f32[2,1,1536]{2,1,0:T(1,128)}, u32[]{:S(2)}) copy-start(f32[2,1,1536]{2,1,0:T(1,128)} %param.13) | copy-start | bytes 36868
  87.3 21.2 %copy-start.7 = (f32[2,1,1536]{2,1,0:T(1,128)S(1)}, f32[2,1,1536]{2,1,0:T(1,128)}, u32[]{:S(2)}) copy-start(f32[2,1,1536]{2,1,0:T(1,128)} %param.14) | copy-start | bytes 36868
Sparse Core Ops, SparseCore 0:
  42.1 45.7 reduce-scatter.4
where the time goes:
time: 189 us; the launch traced here: 188 us
  blocking collectives  109 us (58%)
  local copies, waits for them, and re-layouts  53.2 us (28%)
  between operations  14.9 us (8%)
  other arithmetic  10.4 us (6%)
    all_gather x1, blocking collectives, shards(): whole_block = lax.all_gather(sent_a, ('roll', 'tp'), axis=1, tiled=True)  54.8 us
    unnamed x25, local copies, waits for them, and re-layouts  40.3 us
    unnamed x1, blocking collectives  26.1 us
    all_gather x1, blocking collectives, shards(): lax.all_gather(tensor_ranks, 'tp', axis=1, tiled=True)  15.6 us
    all_gather x1, blocking collectives, shards(): tensor_ranks = lax.all_gather(sent_b, 'dp', axis=1, tiled=True)  12.8 us
    div x2, local copies, waits for them, and re-layouts, requantize(): combined_weight / block_peak[:, :, None, :, None]  6.27 us
    convert_element_type x1, other arithmetic, requantize(): requantized = (combined_weight / block_peak[:, :, None, :, None]).astype(...  4.56 us
  transfers between devices with their start and end apart: 1, of which 0 were waited for; matrix products, arithmetic and copies ran while one was open for 4% of the time, Pallas kernels for 0%

commit v1 on v0

v1 whole, which is shorter than its diff:
```python
import jax
import jax.numpy as jnp
from jax import lax
from jax.experimental import pallas as pl
from jax.experimental.pallas import tpu as pltpu
from jax.sharding import PartitionSpec as P

QBLK = 128
STEP = 100
LANES = 128
adapter_scale = 0.5
learn_rate = 0.05


def adam(param, gradient, first, second):
    first_new = 0.9 * first + 0.1 * gradient
    second_new = 0.999 * second + 0.001 * gradient * gradient
    corr_one = 1.0 - 0.9**STEP
    corr_two = 1.0 - 0.999**STEP
    param_new = param - learn_rate * (first_new / corr_one) / (
        jnp.sqrt(second_new / corr_two) + 1e-08
    )
    return param_new, first_new, second_new


def vmem(n):
    return [pl.BlockSpec(memory_space=pltpu.VMEM)] * n


def pack_kernel(ga_ref, gb_ref, m_ref, scr):
    scr[:, :, 768:896] = jnp.zeros((8, 8, 128), jnp.float32)
    for l in range(2):
        for j in range(3):
            for d in range(8):
                scr[d, 4 * l : 4 * l + 4, 128 * j : 128 * j + 128] = ga_ref[
                    l, pl.ds(12 * d + j, 4, stride=3), :
                ]
        for d in range(8):
            scr[d, 4 * l : 4 * l + 2, 384:896] = gb_ref[0, l, 2 * d : 2 * d + 2, 0:512]
            scr[d, 4 * l + 2 : 4 * l + 4, 384:768] = gb_ref[0, l, 2 * d : 2 * d + 2, 512:896]
    m_ref[...] = scr[...].astype(jnp.bfloat16)


def adam_kernel(
    r_ref, pa, ma, va, pb, mb, vb, oa, oma, ova, ob, omb, ovb, sa_ref, sb_ref, asc, bsc
):
    total = r_ref[0].astype(jnp.float32)
    for d in range(1, 8):
        total = total + r_ref[d].astype(jnp.float32)
    asc[...] = jnp.zeros((4, 8, 128), jnp.float32)
    for j in range(3):
        rows = pl.ds(j, 8, stride=3)
        p, m, v = adam(pa[rows, :], total[:, 128 * j : 128 * j + 128], ma[rows, :], va[rows, :])
        oa[rows, :] = p
        oma[rows, :] = m
        ova[rows, :] = v
        for l in range(2):
            for t in range(4):
                asc[t, 3 * l + j : 3 * l + j + 1, :] = p[4 * l + t : 4 * l + t + 1, :]
    block = asc[...].astype(jnp.bfloat16)
    for r in range(16):
        sa_ref[4 * r : 4 * r + 4] = block
    bsc[...] = jnp.zeros((8, 512), jnp.float32)
    for l in range(2):
        for h, (lo, hi) in enumerate(((0, 512), (512, 896))):
            rows = slice(4 * l + 2 * h, 4 * l + 2 * h + 2)
            p, m, v = adam(
                pb[l, :, lo:hi],
                total[rows, 384 : 384 + hi - lo],
                mb[l, :, lo:hi],
                vb[l, :, lo:hi],
            )
            ob[l, :, lo:hi] = p
            omb[l, :, lo:hi] = m
            ovb[l, :, lo:hi] = v
            bsc[rows, 0 : hi - lo] = p
    block = bsc[...].astype(jnp.bfloat16)
    for i in range(32):
        sb_ref[i] = block


def merge_kernel(ra_ref, rb_ref, codes_ref, scale_ref, out_ref, peak_ref, asc, bsc):
    asc[...] = ra_ref[...].astype(jnp.float32).reshape(512, 128)
    for q in range(4):
        bsc[q] = rb_ref[:, :, 128 * q : 128 * q + 128].astype(jnp.float32).reshape(256, 128)
    lane = lax.broadcasted_iota(jnp.int32, (1, 7), 1)
    for l in range(2):
        halves = []
        for h, width in enumerate((512, 384)):
            row = 4 * l + 2 * h
            tiles = [
                jnp.concatenate(
                    [bsc[q, pl.ds(row + k, 32, stride=8), :] for k in range(2)], axis=0
                )
                for q in range(width // QBLK)
            ]
            halves.append(jnp.concatenate(tiles, axis=1).astype(jnp.bfloat16))
        for j in range(3):
            row = 3 * l + j
            left = jnp.concatenate(
                [asc[pl.ds(8 * k + row, 32, stride=16), :] for k in range(2)], axis=0
            )
            left = (adapter_scale * left).astype(jnp.bfloat16)
            peaks = jnp.zeros((1, 7), jnp.float32)
            for h, width in enumerate((512, 384)):
                product = lax.dot_general(
                    left,
                    halves[h],
                    (((0,), (0,)), ((), ())),
                    preferred_element_type=jnp.float32,
                )
                for c in range(width // QBLK):
                    block = 4 * h + c
                    rows = slice(QBLK * j, QBLK * j + QBLK)
                    cols = slice(QBLK * block, QBLK * block + QBLK)
                    scale = scale_ref[j, l : l + 1, block : block + 1]
                    merged = (
                        codes_ref[l, rows, cols].astype(jnp.float32) * scale
                        + product[:, QBLK * c : QBLK * c + QBLK]
                    )
                    peak = (
                        jnp.max(
                            jnp.max(jnp.abs(merged), axis=0, keepdims=True), axis=1, keepdims=True
                        )
                        + 1e-06
                    )
                    out_ref[l, rows, cols] = (merged * (1.0 / peak)).astype(jnp.bfloat16)
                    peaks = jnp.where(lane == block, peak, peaks)
            peak_ref[j, l : l + 1, :] = peaks


def shards(ga, gb, pa, ma, va, pb, mb, vb, codes, scales):
    f32, bf16 = jnp.float32, jnp.bfloat16
    sds = jax.ShapeDtypeStruct
    messages = pl.pallas_call(
        pack_kernel,
        out_shape=sds((8, 8, 896), bf16),
        in_specs=vmem(2),
        out_specs=vmem(1)[0],
        scratch_shapes=[pltpu.VMEM((8, 8, 896), f32)],
        name="pack",
    )(ga.reshape(2, 96, 128), gb)
    received = lax.all_to_all(messages, "dp", 0, 0, tiled=True)
    flat = [a.reshape(24, 128) for a in (pa, ma, va)]
    oa, oma, ova, ob, omb, ovb, send_a, send_b = pl.pallas_call(
        adam_kernel,
        out_shape=[sds((24, 128), f32)] * 3
        + [sds((2, 2, 896), f32)] * 3
        + [sds((64, 8, 128), bf16), sds((32, 8, 512), bf16)],
        in_specs=vmem(7),
        out_specs=vmem(8),
        scratch_shapes=[pltpu.VMEM((4, 8, 128), f32), pltpu.VMEM((8, 512), f32)],
        name="adam",
    )(received, *flat, pb, mb, vb)
    all_a = lax.all_to_all(send_a, ("roll", "tp"), 0, 0, tiled=True)
    all_b = lax.all_to_all(send_b, ("tp", "dp"), 0, 0, tiled=True)
    out, peaks = pl.pallas_call(
        merge_kernel,
        out_shape=[sds((2, 384, 896), bf16), sds((3, 2, 7), f32)],
        in_specs=vmem(4),
        out_specs=vmem(2),
        scratch_shapes=[pltpu.VMEM((512, 128), f32), pltpu.VMEM((4, 256, 128), f32)],
        compiler_params=pltpu.CompilerParams(vmem_limit_bytes=32 * 1024 * 1024),
        name="merge",
    )(all_a, all_b, codes, scales.transpose(1, 0, 2))
    return (
        out,
        peaks.transpose(1, 0, 2),
        oa.reshape(2, 1, 1536),
        oma.reshape(2, 1, 1536),
        ova.reshape(2, 1, 1536),
        ob,
        omb,
        ovb,
    )


def solution(mesh):
    in_specs = (
        P("dp", None, ("roll", "tp"), None),
        P("dp", None, "tp", "roll"),
        P(None, ("roll", "tp"), "dp"),
        P(None, ("roll", "tp"), "dp"),
        P(None, ("roll", "tp"), "dp"),
        P(None, ("tp", "dp"), "roll"),
        P(None, ("tp", "dp"), "roll"),
        P(None, ("tp", "dp"), "roll"),
        P(None, ("dp", "tp"), "roll"),
        P(None, ("dp", "tp"), "roll"),
    )
    out_specs = (
        P(None, ("dp", "tp"), "roll"),
        P(None, ("dp", "tp"), "roll"),
        P(None, ("roll", "tp"), "dp"),
        P(None, ("roll", "tp"), "dp"),
        P(None, ("roll", "tp"), "dp"),
        P(None, ("tp", "dp"), "roll"),
        P(None, ("tp", "dp"), "roll"),
        P(None, ("tp", "dp"), "roll"),
    )
    return jax.shard_map(shards, mesh=mesh, in_specs=in_specs, out_specs=out_specs, check_vma=False)
```

time: 189 us -> 62.7 us (0.33)
  the two profiles are of different devices: /device:TPU:16 before, /device:TPU:1 now
where the time goes in v1:
time: 62.7 us; the launch traced here: 62.3 us
  blocking collectives  55.9 us (89%)
  Pallas kernels  5.79 us (9%)
  between operations  0.65 us (1%)
    all_to_all x1, blocking collectives, shards(): all_a = lax.all_to_all(send_a, ('roll', 'tp'), 0, 0, tiled=True)  23 us
    all_to_all x1, blocking collectives, shards(): all_b = lax.all_to_all(send_b, ('tp', 'dp'), 0, 0, tiled=True)  16.9 us
    all_to_all x1, blocking collectives, shards(): received = lax.all_to_all(messages, 'dp', 0, 0, tiled=True)  16 us
    pallas_call x1, Pallas kernels, shards(): pl.pallas_call(merge_kernel, out_shape=[sds((2, 384, 896), bf16), sds((3,...  2.23 us
    pallas_call x1, Pallas kernels, shards(): pl.pallas_call(pack_kernel, out_shape=sds((8, 8, 896), bf16), in_specs=vm...  1.79 us
    pallas_call x1, Pallas kernels, shards(): pl.pallas_call(adam_kernel, out_shape=[sds((24, 128), f32)] * 3 + [sds((2...  1.77 us

profile of v1, /device:TPU:1, one launch (start us, length us, event | category | flops | bytes accessed | tf_op | source)
XLA Modules:
  0.0 62.3 jit_solution(5624316318482485718)
XLA Ops:
  0.6 0.0 copy-start.1
  0.6 0.0 copy-start
  0.7 1.8 %pack.1 = bf16[8,8,896]{2,1,0:T(8,128)(2,1)} custom-call(f32[2,96,128]{2,1,0:T(8,128)} %bitcast.10, f32[1,2,16,896]{3,2,1,0:T(8,128)} %gb_ref.1), custom_call_target="tpu_custom_call" | custom-call | tf_op jit(solution)/shard_map/pack/pallas_call | solution.py:135
  2.4 16.0 %all_to_all.15.r_ref = bf16[8,8,896]{2,1,0:T(8,128)(2,1)} all-to-all(bf16[8,8,896]{2,1,0:T(8,128)(2,1)} %pack.1), channel_id=1, replica_groups=mesh['dp'=8,'roll'=16,'tp'=4] {'dp'}, dimensions={0} | all-to-all | bytes 229376 | tf_op jit(solution)/shard_map/all_to_all | solution.py:143
  18.4 1.8 %adam.1 = (f32[24,128]{1,0:T(8,128)}, f32[24,128]{1,0:T(8,128)}, f32[24,128]{1,0:T(8,128)}, f32[2,2,896]{2,1,0:T(2,128)}, f32[2,2,896]{2,1,0:T(2,128)}, /*index=...) custom-call(bf16[8,8,896]{2,1,0:T(8,128)(2,1)} %all_to_all.15.r_ref, f32[24,128]{1,0:T(8,128)} %bitcast.11, ...), custom_call_target="tpu_custom_call" | custom-call | tf_op jit(solution)/shard_map/adam/pallas_call | solution.py:145
  20.2 23.0 %all_to_all.16.ra_ref = bf16[64,8,128]{2,1,0:T(8,128)(2,1)S(1)} all-to-all(bf16[64,8,128]{2,1,0:T(8,128)(2,1)} %get-tuple-element.18), channel_id=1, replica_groups=mesh['dp'=8,'roll'=16,'tp'=4] {'roll','tp'}, dimensions={0} | all-to-all | bytes 262144 | tf_op jit(solution)/shard_map/all_to_all | solution.py:155
  43.2 16.9 %all_to_all.17.rb_ref = bf16[32,8,512]{2,1,0:T(8,128)(2,1)S(1)} all-to-all(bf16[32,8,512]{2,1,0:T(8,128)(2,1)} %get-tuple-element.19), channel_id=1, replica_groups=mesh['dp'=8,'roll'=16,'tp'=4] {'tp','dp'}, dimensions={0} | all-to-all | bytes 524288 | tf_op jit(solution)/shard_map/all_to_all | solution.py:156
  60.1 0.0 copy-done.1
  60.1 0.0 copy-done
  60.1 2.2 %merge.1 = (bf16[2,384,896]{2,1,0:T(8,128)(2,1)}, f32[3,2,7]{2,1,0:T(2,128)}) custom-call(bf16[64,8,128]{2,1,0:T(8,128)(2,1)S(1)} %all_to_all.16.ra_ref, bf16[32,8,512]{2,1,0:T(8,128)(2,1)S(1)} %all_to_all.17.rb_ref, bf16[2,384,896]{2,1,0:T(8,128)(2,1)S(1)} %copy-done, f32[3,2,7]{2,1,0:T(2,128)S(1)} %bitcast.9), custom_call_target="tpu_custom_call" | custom-call | tf_op jit(solution)/shard_map/merge/pallas_call | solution.py:157
Async XLA Ops:
  0.6 59.5 %copy-start.1 = (f32[2,3,7]{2,0,1:T(2,128)S(1)}, f32[2,3,7]{2,0,1:T(2,128)}, u32[]{:S(2)}) copy-start(f32[2,3,7]{2,0,1:T(2,128)} %param.19) | copy-start | bytes 508
  0.6 59.5 %copy-start = (bf16[2,384,896]{2,1,0:T(8,128)(2,1)S(1)}, bf16[2,384,896]{2,1,0:T(8,128)(2,1)}, u32[]{:S(2)}) copy-start(bf16[2,384,896]{2,1,0:T(8,128)(2,1)} %codes_ref.1) | copy-start | bytes 4128772

commit v2 on v1

--- a/solution.py
+++ b/solution.py
@@ -7,9 +7,9 @@
 
 QBLK = 128
 STEP = 100
-LANES = 128
 adapter_scale = 0.5
 learn_rate = 0.05
+SMALL = pltpu.CompilerParams(vmem_limit_bytes=16 * 1024 * 1024)
 
 
 def adam(param, gradient, first, second):
@@ -27,7 +27,16 @@
     return [pl.BlockSpec(memory_space=pltpu.VMEM)] * n
 
 
-def pack_kernel(ga_ref, gb_ref, m_ref, scr):
+def hbm(n):
+    return [pl.BlockSpec(memory_space=pltpu.HBM)] * n
+
+
+def first_kernel(o_ref):
+    o_ref[...] = jnp.zeros((8, 128), jnp.float32)
+
+
+def pack_kernel(ga_ref, gb_ref, order_ref, m_ref, scr):
+    del order_ref
     scr[:, :, 768:896] = jnp.zeros((8, 8, 128), jnp.float32)
     for l in range(2):
         for j in range(3):
@@ -41,12 +50,11 @@
     m_ref[...] = scr[...].astype(jnp.bfloat16)
 
 
-def adam_kernel(
-    r_ref, pa, ma, va, pb, mb, vb, oa, oma, ova, ob, omb, ovb, sa_ref, sb_ref, asc, bsc
-):
-    total = r_ref[0].astype(jnp.float32)
+def adam_a_kernel(r_ref, pa, ma, va, order_ref, oa, oma, ova, sa_ref, asc):
+    del order_ref
+    total = r_ref[0, :, 0:384].astype(jnp.float32)
     for d in range(1, 8):
-        total = total + r_ref[d].astype(jnp.float32)
+        total = total + r_ref[d, :, 0:384].astype(jnp.float32)
     asc[...] = jnp.zeros((4, 8, 128), jnp.float32)
     for j in range(3):
         rows = pl.ds(j, 8, stride=3)
@@ -60,13 +68,19 @@
     block = asc[...].astype(jnp.bfloat16)
     for r in range(16):
         sa_ref[4 * r : 4 * r + 4] = block
+
+
+def adam_b_kernel(r_ref, pb, mb, vb, ob, omb, ovb, sb_ref, bsc):
+    total = r_ref[0, :, 384:896].astype(jnp.float32)
+    for d in range(1, 8):
+        total = total + r_ref[d, :, 384:896].astype(jnp.float32)
     bsc[...] = jnp.zeros((8, 512), jnp.float32)
     for l in range(2):
         for h, (lo, hi) in enumerate(((0, 512), (512, 896))):
             rows = slice(4 * l + 2 * h, 4 * l + 2 * h + 2)
             p, m, v = adam(
                 pb[l, :, lo:hi],
-                total[rows, 384 : 384 + hi - lo],
+                total[rows, 0 : hi - lo],
                 mb[l, :, lo:hi],
                 vb[l, :, lo:hi],
             )
@@ -75,22 +89,39 @@
             ovb[l, :, lo:hi] = v
             bsc[rows, 0 : hi - lo] = p
     block = bsc[...].astype(jnp.bfloat16)
-    for i in range(32):
+    for i in range(8):
         sb_ref[i] = block
 
 
-def merge_kernel(ra_ref, rb_ref, codes_ref, scale_ref, out_ref, peak_ref, asc, bsc):
+def merge_kernel(ra_ref, b0, b1, b2, b3, codes_ref, scale_ref, *refs):
+    state_in, out_hbm, peak_ref, state_out = refs[:6], refs[6], refs[7], refs[8:14]
+    out_ref, asc, bsc, sems = refs[14:]
+    states = [
+        pltpu.make_async_copy(a, b, sems.at[6 + i])
+        for i, (a, b) in enumerate(zip(state_in, state_out))
+    ]
+    for copy in states:
+        copy.start()
     asc[...] = ra_ref[...].astype(jnp.float32).reshape(512, 128)
-    for q in range(4):
-        bsc[q] = rb_ref[:, :, 128 * q : 128 * q + 128].astype(jnp.float32).reshape(256, 128)
+    for i, b_ref in enumerate((b0, b1, b2, b3)):
+        for q in range(4):
+            bsc[i, q] = b_ref[:, :, 128 * q : 128 * q + 128].astype(jnp.float32).reshape(64, 128)
+    me = lax.axis_index("tp")
+    peers = [lax.rem(me + 4 - i, 4) for i in range(4)]
     lane = lax.broadcasted_iota(jnp.int32, (1, 7), 1)
+    copies = []
     for l in range(2):
         halves = []
         for h, width in enumerate((512, 384)):
             row = 4 * l + 2 * h
             tiles = [
                 jnp.concatenate(
-                    [bsc[q, pl.ds(row + k, 32, stride=8), :] for k in range(2)], axis=0
+                    [
+                        bsc[i, q, pl.ds(row + k, 8, stride=8), :]
+                        for i in range(4)
+                        for k in range(2)
+                    ],
+                    axis=0,
                 )
                 for q in range(width // QBLK)
             ]
@@ -98,10 +129,16 @@
         for j in range(3):
             row = 3 * l + j
             left = jnp.concatenate(
-                [asc[pl.ds(8 * k + row, 32, stride=16), :] for k in range(2)], axis=0
+                [
+                    asc[pl.ds(128 * peers[i] + 8 * k + row, 8, stride=16), :]
+                    for i in range(4)
+                    for k in range(2)
+                ],
+                axis=0,
             )
             left = (adapter_scale * left).astype(jnp.bfloat16)
             peaks = jnp.zeros((1, 7), jnp.float32)
+            rows = slice(QBLK * j, QBLK * j + QBLK)
             for h, width in enumerate((512, 384)):
                 product = lax.dot_general(
                     left,
@@ -111,7 +148,6 @@
                 )
                 for c in range(width // QBLK):
                     block = 4 * h + c
-                    rows = slice(QBLK * j, QBLK * j + QBLK)
                     cols = slice(QBLK * block, QBLK * block + QBLK)
                     scale = scale_ref[j, l : l + 1, block : block + 1]
                     merged = (
@@ -127,51 +163,89 @@
                     out_ref[l, rows, cols] = (merged * (1.0 / peak)).astype(jnp.bfloat16)
                     peaks = jnp.where(lane == block, peak, peaks)
             peak_ref[j, l : l + 1, :] = peaks
+            copies.append(
+                pltpu.make_async_copy(
+                    out_ref.at[l, rows, :], out_hbm.at[l, rows, :], sems.at[row]
+                )
+            )
+            copies[-1].start()
+    for copy in states + copies:
+        copy.wait()
 
 
 def shards(ga, gb, pa, ma, va, pb, mb, vb, codes, scales):
     f32, bf16 = jnp.float32, jnp.bfloat16
     sds = jax.ShapeDtypeStruct
+    a_state = [sds((24, 128), f32)] * 3
+    b_state = [sds((2, 2, 896), f32)] * 3
+    pa, ma, va = (a.reshape(24, 128) for a in (pa, ma, va))
+    first = pl.pallas_call(
+        first_kernel,
+        out_shape=sds((8, 128), f32),
+        out_specs=vmem(1)[0],
+        compiler_params=SMALL,
+        cost_estimate=pl.CostEstimate(flops=10**9, bytes_accessed=4096, transcendentals=0),
+        name="first",
+    )()
     messages = pl.pallas_call(
         pack_kernel,
         out_shape=sds((8, 8, 896), bf16),
-        in_specs=vmem(2),
+        in_specs=vmem(3),
         out_specs=vmem(1)[0],
         scratch_shapes=[pltpu.VMEM((8, 8, 896), f32)],
+        compiler_params=SMALL,
+        cost_estimate=pl.CostEstimate(flops=10**9, bytes_accessed=400000, transcendentals=0),
         name="pack",
-    )(ga.reshape(2, 96, 128), gb)
+    )(ga.reshape(2, 96, 128), gb, first)
     received = lax.all_to_all(messages, "dp", 0, 0, tiled=True)
-    flat = [a.reshape(24, 128) for a in (pa, ma, va)]
-    oa, oma, ova, ob, omb, ovb, send_a, send_b = pl.pallas_call(
-        adam_kernel,
-        out_shape=[sds((24, 128), f32)] * 3
-        + [sds((2, 2, 896), f32)] * 3
-        + [sds((64, 8, 128), bf16), sds((32, 8, 512), bf16)],
-        in_specs=vmem(7),
-        out_specs=vmem(8),
-        scratch_shapes=[pltpu.VMEM((4, 8, 128), f32), pltpu.VMEM((8, 512), f32)],
-        name="adam",
-    )(received, *flat, pb, mb, vb)
+    pb, mb, vb, send_b = pl.pallas_call(
+        adam_b_kernel,
+        out_shape=b_state + [sds((8, 8, 512), bf16)],
+        in_specs=vmem(4),
+        out_specs=vmem(4),
+        scratch_shapes=[pltpu.VMEM((8, 512), f32)],
+        compiler_params=SMALL,
+        cost_estimate=pl.CostEstimate(flops=100000, bytes_accessed=400000, transcendentals=3584),
+        name="adam_b",
+    )(received, pb, mb, vb)
+    all_b = [lax.all_to_all(send_b, "dp", 0, 0, tiled=True)]
+    pa, ma, va, send_a = pl.pallas_call(
+        adam_a_kernel,
+        out_shape=a_state + [sds((64, 8, 128), bf16)],
+        in_specs=vmem(5),
+        out_specs=vmem(4),
+        scratch_shapes=[pltpu.VMEM((4, 8, 128), f32)],
+        compiler_params=SMALL,
+        cost_estimate=pl.CostEstimate(flops=100000, bytes_accessed=200000, transcendentals=3072),
+        name="adam_a",
+    )(received, pa, ma, va, send_b)
+    all_b[0], send_a = lax.optimization_barrier((all_b[0], send_a))
     all_a = lax.all_to_all(send_a, ("roll", "tp"), 0, 0, tiled=True)
-    all_b = lax.all_to_all(send_b, ("tp", "dp"), 0, 0, tiled=True)
-    out, peaks = pl.pallas_call(
+    for shift in range(1, 4):
+        all_b.append(lax.ppermute(all_b[0], "tp", [(i, (i + shift) % 4) for i in range(4)]))
+    out, peaks, pa, ma, va, pb, mb, vb = pl.pallas_call(
         merge_kernel,
-        out_shape=[sds((2, 384, 896), bf16), sds((3, 2, 7), f32)],
-        in_specs=vmem(4),
-        out_specs=vmem(2),
-        scratch_shapes=[pltpu.VMEM((512, 128), f32), pltpu.VMEM((4, 256, 128), f32)],
-        compiler_params=pltpu.CompilerParams(vmem_limit_bytes=32 * 1024 * 1024),
+        out_shape=[sds((2, 384, 896), bf16), sds((3, 2, 7), f32)] + a_state + b_state,
+        in_specs=vmem(13),
+        out_specs=hbm(1) + vmem(1) + hbm(6),
+        scratch_shapes=[
+            pltpu.VMEM((2, 384, 896), bf16),
+            pltpu.VMEM((512, 128), f32),
+            pltpu.VMEM((4, 4, 64, 128), f32),
+            pltpu.SemaphoreType.DMA((12,)),
+        ],
+        compiler_params=SMALL,
         name="merge",
-    )(all_a, all_b, codes, scales.transpose(1, 0, 2))
+    )(all_a, *all_b, codes, scales.transpose(1, 0, 2), pa, ma, va, pb, mb, vb)
     return (
         out,
         peaks.transpose(1, 0, 2),
-        oa.reshape(2, 1, 1536),
-        oma.reshape(2, 1, 1536),
-        ova.reshape(2, 1, 1536),
-        ob,
-        omb,
-        ovb,
+        pa.reshape(2, 1, 1536),
+        ma.reshape(2, 1, 1536),
+        va.reshape(2, 1, 1536),
+        pb,
+        mb,
+        vb,
     )
 
 

time: 62.7 us -> 55.3 us (0.88)
  blocking collectives: 55.9 us -> 14.5 us
  starting transfers between devices: 0 us -> 25.8 us
  waiting for transfers between devices: 0 us -> 7.67 us
  Pallas kernels: 5.79 us -> 4.8 us
  local copies, waits for them, and re-layouts: 0.01 us -> 0.96 us
    all_to_all x2 -> x0, blocking collectives: 39.9 us -> none  [the longest x1 23 us: shards(): all_a = lax.all_to_all(send_a, ('roll', 'tp'), 0, 0, tiled=True)]
    all_to_all x0 -> x2, starting transfers between devices: none -> 16.7 us  [the longest x1 12.7 us: shards(): all_a = lax.all_to_all(send_a, ('roll', 'tp'), 0, 0, tiled=True)]
    ppermute x0 -> x3, starting transfers between devices: none -> 9.1 us  [shards(): lax.ppermute(all_b[0], 'tp', [(i, (i + shift) % 4) for i in range(4)])]
    ppermute x0 -> x3, waiting for transfers between devices: none -> 4.38 us  [shards(): lax.ppermute(all_b[0], 'tp', [(i, (i + shift) % 4) for i in range(4)])]
    all_to_all x0 -> x2, waiting for transfers between devices: none -> 3.3 us  [the longest x1 3.29 us: shards(): all_b = [lax.all_to_all(send_b, 'dp', 0, 0, tiled=True)]]
    pallas_call x1, Pallas kernels: 1.79 us -> 0.09 us  [shards(): pl.pallas_call(pack_kernel, out_shape=sds((8, 8, 896), bf16), in_specs=vm...]
    all_to_all x1, blocking collectives: 16 us -> 14.5 us  [shards(): received = lax.all_to_all(messages, 'dp', 0, 0, tiled=True)]
    unnamed x4 -> x20, local copies, waits for them, and re-layouts: 0.01 us -> 0.96 us
  transfers between devices with their start and end apart: 0 -> 5, of which waited for: 0 -> 3; matrix products, arithmetic and copies ran while one was open for 0% -> 0% of each run, Pallas kernels for 0% -> 3%
where the time goes in v2:
time: 55.3 us; the launch traced here: 54.5 us
  starting transfers between devices  25.8 us (47%)
  blocking collectives  14.5 us (26%)
  waiting for transfers between devices  7.67 us (14%)
  Pallas kernels  4.8 us (9%)
  local copies, waits for them, and re-layouts  0.96 us (2%)
  between operations  0.76 us (1%)
    all_to_all x1, blocking collectives, shards(): received = lax.all_to_all(messages, 'dp', 0, 0, tiled=True)  14.5 us
    all_to_all x1, starting transfers between devices, shards(): all_a = lax.all_to_all(send_a, ('roll', 'tp'), 0, 0, tiled=True)  12.7 us
    ppermute x3, starting transfers between devices, shards(): lax.ppermute(all_b[0], 'tp', [(i, (i + shift) % 4) for i in range(4)])  9.1 us
    ppermute x3, waiting for transfers between devices, shards(): lax.ppermute(all_b[0], 'tp', [(i, (i + shift) % 4) for i in range(4)])  4.38 us
    all_to_all x1, starting transfers between devices, shards(): all_b = [lax.all_to_all(send_b, 'dp', 0, 0, tiled=True)]  4.09 us
    all_to_all x1, waiting for transfers between devices, shards(): all_b = [lax.all_to_all(send_b, 'dp', 0, 0, tiled=True)]  3.29 us
    pallas_call x1, Pallas kernels, shards(): pl.pallas_call(merge_kernel, out_shape=[sds((2, 384, 896), bf16), sds((3,...  2.47 us
    pallas_call x1, Pallas kernels, shards(): pl.pallas_call(adam_a_kernel, out_shape=a_state + [sds((64, 8, 128), bf16...  1.56 us
  transfers between devices with their start and end apart: 5, of which 3 were waited for; matrix products, arithmetic and copies ran while one was open for 0% of the time, Pallas kernels for 3%

profile of v2, /device:TPU:1, one launch (start us, length us, event | category | flops | bytes accessed | tf_op | source)
XLA Modules:
  0.0 54.5 jit_solution(6446051356697563025)
XLA Ops:
  0.6 0.0 copy-start.8
  0.6 0.0 copy-start.9
  0.7 0.9 %copy-done.8 = f32[1,2,16,896]{3,2,1,0:T(8,128)S(1)} copy-done((f32[1,2,16,896]{3,2,1,0:T(8,128)S(1)}, f32[1,2,16,896]{3,2,1,0:T(8,128)}, u32[]{:S(2)}) %copy-start.8) | copy-done | bytes 114712
  1.5 0.1 copy-done.9
  1.6 0.0 copy-start.1
  1.6 0.0 copy-start.2
  1.6 0.0 copy-start.3
  1.6 0.0 copy-start.4
  1.6 0.0 copy-start.5
  1.6 0.0 copy-start.6
  1.6 0.0 copy-start
  1.6 0.0 copy-start.7
  1.6 0.1 pack.1
  1.7 14.5 %all_to_all.15.r_ref = bf16[8,8,896]{2,1,0:T(8,128)(2,1)S(1)} all-to-all(bf16[8,8,896]{2,1,0:T(8,128)(2,1)S(1)} %pack.1), channel_id=1, replica_groups=mesh['dp'=8,'roll'=16,'tp'=4] {'dp'}, dimensions={0} | all-to-all | bytes 229376 | tf_op jit(solution)/shard_map/all_to_all | solution.py:200
  16.2 0.0 copy-done.1
  16.2 0.0 copy-done.2
  16.2 0.0 copy-done.3
  16.3 0.7 %adam_b.1 = (f32[2,2,896]{2,1,0:T(2,128)S(1)}, f32[2,2,896]{2,1,0:T(2,128)S(1)}, f32[2,2,896]{2,1,0:T(2,128)S(1)}, bf16[8,8,512]{2,1,0:T(8,128)(2,1)}) custom-call(bf16[8,8,896]{2,1,0:T(8,128)(2,1)S(1)} %all_to_all.15.r_ref, f32[2,2,896]{2,1,0:T(2,128)S(1)} %copy-done.1, f32[2,2,896]{2,1,0:T(2,128)S(1)} %copy-done.2, f32[2,2,896]{2,1,0:T(2,128)S(1)} %copy-done.3), custom_call_target="tpu_custom_call" | custom-call | flops 100000 | bytes 400000 | tf_op jit(solution)/shard_map/adam_b/pallas_call | solution.py:201
  16.9 4.1 %all-to-all-start.1 = ((bf16[8,8,512]{2,1,0:T(8,128)(2,1)}), bf16[8,8,512]{2,1,0:T(8,128)(2,1)S(1)}, u32[]{:S(2)}, u32[]{:S(2)}) async-start(bf16[8,8,512]{2,1,0:T(8,128)(2,1)} %get-tuple-element.26.order_ref), calls=%async_computation.1 | async-start | bytes 131072 | tf_op jit(solution)/shard_map/all_to_all | solution.py:211
  21.0 0.0 copy-done.4
  21.0 0.0 copy-done.5
  21.0 0.0 copy-done.6
  21.0 1.6 %adam_a.1 = (f32[24,128]{1,0:T(8,128)S(1)}, f32[24,128]{1,0:T(8,128)S(1)}, f32[24,128]{1,0:T(8,128)S(1)}, bf16[64,8,128]{2,1,0:T(8,128)(2,1)}) custom-call(bf16[8,8,896]{2,1,0:T(8,128)(2,1)S(1)} %all_to_all.15.r_ref, f32[24,128]{1,0:T(8,128)S(1)} %bitcast.9, f32[24,128]{1,0:T(8,128)S(1)} %bitcast.10, f32[24,128]{1,0:T(8,128)S(1)} %bitcast.11, ...), custom_call_target="tpu_custom_call" | custom-call | flops 100000 | bytes 200000 | tf_op jit(solution)/shard_map/adam_a/pallas_call | solution.py:212
  22.6 3.3 %all-to-all-done.1.b0 = bf16[8,8,512]{2,1,0:T(8,128)(2,1)S(1)} async-done(((bf16[8,8,512]{2,1,0:T(8,128)(2,1)}), bf16[8,8,512]{2,1,0:T(8,128)(2,1)S(1)}, u32[]{:S(2)}, u32[]{:S(2)}) %all-to-all-start.1) | async-done | bytes 65568 | tf_op jit(solution)/shard_map/all_to_all | solution.py:211
  25.9 12.7 %all-to-all-start.2 = ((bf16[64,8,128]{2,1,0:T(8,128)(2,1)}), bf16[64,8,128]{2,1,0:T(8,128)(2,1)S(1)}, u32[]{:S(2)}, u32[]{:S(2)}) async-start(bf16[64,8,128]{2,1,0:T(8,128)(2,1)} %get-tuple-element.28), calls=%async_computation.2 | async-start | bytes 262144 | tf_op jit(solution)/shard_map/all_to_all | solution.py:223
  38.6 4.7 %collective-permute-start.2 = (bf16[8,8,512]{2,1,0:T(8,128)(2,1)S(1)}, bf16[8,8,512]{2,1,0:T(8,128)(2,1)S(1)}, u32[]{:S(2)}, u32[]{:S(2)}) collective-permute-start(bf16[8,8,512]{2,1,0:T(8,128)(2,1)S(1)} %all-to-all-done.1.b0), channel_id=1, source_target_pairs={{0,3},{1,0},{2,1},{3,2},{4,7},{5,4},{6,5},{7,6},{8,11},{9,8},{10,9... | collective-permute-start | bytes 196616 | tf_op jit(solution)/shard_map/ppermute | solution.py:225
  43.3 1.9 %collective-permute-start.1 = (bf16[8,8,512]{2,1,0:T(8,128)(2,1)S(1)}, bf16[8,8,512]{2,1,0:T(8,128)(2,1)S(1)}, u32[]{:S(2)}, u32[]{:S(2)}) collective-permute-start(bf16[8,8,512]{2,1,0:T(8,128)(2,1)S(1)} %all-to-all-done.1.b0), channel_id=1, source_target_pairs={{0,2},{1,3},{2,0},{3,1},{4,6},{5,7},{6,4},{7,5},{8,10},{9,11},{10,... | collective-permute-start | bytes 196616 | tf_op jit(solution)/shard_map/ppermute | solution.py:225
  45.2 2.5 %collective-permute-start = (bf16[8,8,512]{2,1,0:T(8,128)(2,1)S(1)}, bf16[8,8,512]{2,1,0:T(8,128)(2,1)S(1)}, u32[]{:S(2)}, u32[]{:S(2)}) collective-permute-start(bf16[8,8,512]{2,1,0:T(8,128)(2,1)S(1)} %all-to-all-done.1.b0), channel_id=1, source_target_pairs={{0,1},{1,2},{2,3},{3,0},{4,5},{5,6},{6,7},{7,4},{8,9},{9,10},{10,1... | collective-permute-start | bytes 196616 | tf_op jit(solution)/shard_map/ppermute | solution.py:225
  47.7 0.0 collective-permute-done.2.b3
  47.7 2.5 %collective-permute-done.1.b2 = bf16[8,8,512]{2,1,0:T(8,128)(2,1)S(1)} collective-permute-done((bf16[8,8,512]{2,1,0:T(8,128)(2,1)S(1)}, bf16[8,8,512]{2,1,0:T(8,128)(2,1)S(1)}, u32[]{:S(2)}, u32[]{:S(2)}) %collective-permute-start.1) | collective-permute-done | bytes 65568 | tf_op jit(solution)/shard_map/ppermute | solution.py:225
  50.2 1.9 %collective-permute-done.b1 = bf16[8,8,512]{2,1,0:T(8,128)(2,1)S(1)} collective-permute-done((bf16[8,8,512]{2,1,0:T(8,128)(2,1)S(1)}, bf16[8,8,512]{2,1,0:T(8,128)(2,1)S(1)}, u32[]{:S(2)}, u32[]{:S(2)}) %collective-permute-start) | collective-permute-done | bytes 65568 | tf_op jit(solution)/shard_map/ppermute | solution.py:225
  52.1 0.0 all-to-all-done.2.ra_ref
  52.1 0.0 copy-done
  52.1 0.0 copy-done.7
  52.1 2.5 %merge.1 = (bf16[2,384,896]{2,1,0:T(8,128)(2,1)}, f32[3,2,7]{2,1,0:T(2,128)}, f32[24,128]{1,0:T(8,128)}, f32[24,128]{1,0:T(8,128)}, f32[24,128]{1,0:T(8,128)}, /...) custom-call(bf16[64,8,128]{2,1,0:T(8,128)(2,1)S(1)} %all-to-all-done.2.ra_ref, ...), custom_call_target="tpu_custom_call" | custom-call | tf_op jit(solution)/shard_map/merge/pallas_call | solution.py:226
  (1 shorter events, 0.0 us)
Async XLA Ops:
  0.6 0.9 %copy-start.8 = (f32[1,2,16,896]{3,2,1,0:T(8,128)S(1)}, f32[1,2,16,896]{3,2,1,0:T(8,128)}, u32[]{:S(2)}) copy-start(f32[1,2,16,896]{3,2,1,0:T(8,128)} %gb_ref.1) | copy-start | bytes 344068
  0.6 0.9 %copy-start.9 = (f32[1,2,1,12288]{3,2,1,0:T(1,128)S(1)}, f32[1,2,1,12288]{3,2,1,0:T(1,128)}, u32[]{:S(2)}) copy-start(f32[1,2,1,12288]{3,2,1,0:T(1,128)} %param.10) | copy-start | bytes 294916
  1.6 14.7 %copy-start.1 = (f32[2,2,896]{2,1,0:T(2,128)S(1)}, f32[2,2,896]{2,1,0:T(2,128)}, u32[]{:S(2)}) copy-start(f32[2,2,896]{2,1,0:T(2,128)} %pb.1) | copy-start | bytes 43012
  1.6 14.7 %copy-start.2 = (f32[2,2,896]{2,1,0:T(2,128)S(1)}, f32[2,2,896]{2,1,0:T(2,128)}, u32[]{:S(2)}) copy-start(f32[2,2,896]{2,1,0:T(2,128)} %mb.1) | copy-start | bytes 43012
  1.6 14.7 %copy-start.3 = (f32[2,2,896]{2,1,0:T(2,128)S(1)}, f32[2,2,896]{2,1,0:T(2,128)}, u32[]{:S(2)}) copy-start(f32[2,2,896]{2,1,0:T(2,128)} %vb.1) | copy-start | bytes 43012
  1.6 19.4 %copy-start.4 = (f32[2,1,1536]{2,1,0:T(1,128)S(1)}, f32[2,1,1536]{2,1,0:T(1,128)}, u32[]{:S(2)}) copy-start(f32[2,1,1536]{2,1,0:T(1,128)} %param.12) | copy-start | bytes 36868
  1.6 19.4 %copy-start.5 = (f32[2,1,1536]{2,1,0:T(1,128)S(1)}, f32[2,1,1536]{2,1,0:T(1,128)}, u32[]{:S(2)}) copy-start(f32[2,1,1536]{2,1,0:T(1,128)} %param.13) | copy-start | bytes 36868
  1.6 19.4 %copy-start.6 = (f32[2,1,1536]{2,1,0:T(1,128)S(1)}, f32[2,1,1536]{2,1,0:T(1,128)}, u32[]{:S(2)}) copy-start(f32[2,1,1536]{2,1,0:T(1,128)} %param.14) | copy-start | bytes 36868
  1.6 50.5 %copy-start = (bf16[2,384,896]{2,1,0:T(8,128)(2,1)S(1)}, bf16[2,384,896]{2,1,0:T(8,128)(2,1)}, u32[]{:S(2)}) copy-start(bf16[2,384,896]{2,1,0:T(8,128)(2,1)} %codes_ref.1) | copy-start | bytes 4128772
  1.6 50.4 %copy-start.7 = (f32[2,3,7]{2,0,1:T(2,128)S(1)}, f32[2,3,7]{2,0,1:T(2,128)}, u32[]{:S(2)}) copy-start(f32[2,3,7]{2,0,1:T(2,128)} %param.19) | copy-start | bytes 508
  16.9 9.0 %all-to-all-start.1 = ((bf16[8,8,512]{2,1,0:T(8,128)(2,1)}), bf16[8,8,512]{2,1,0:T(8,128)(2,1)S(1)}, u32[]{:S(2)}, u32[]{:S(2)}) async-start(bf16[8,8,512]{2,1,0:T(8,128)(2,1)} %get-tuple-element.26.order_ref), calls=%async_computation.1 | async-start | bytes 131072 | tf_op jit(solution)/shard_map/all_to_all | solution.py:211
  25.9 26.2 %all-to-all-start.2 = ((bf16[64,8,128]{2,1,0:T(8,128)(2,1)}), bf16[64,8,128]{2,1,0:T(8,128)(2,1)S(1)}, u32[]{:S(2)}, u32[]{:S(2)}) async-start(bf16[64,8,128]{2,1,0:T(8,128)(2,1)} %get-tuple-element.28), calls=%async_computation.2 | async-start | bytes 262144 | tf_op jit(solution)/shard_map/all_to_all | solution.py:223
  38.6 9.1 %collective-permute-start.2 = (bf16[8,8,512]{2,1,0:T(8,128)(2,1)S(1)}, bf16[8,8,512]{2,1,0:T(8,128)(2,1)S(1)}, u32[]{:S(2)}, u32[]{:S(2)}) collective-permute-start(bf16[8,8,512]{2,1,0:T(8,128)(2,1)S(1)} %all-to-all-done.1.b0), channel_id=1, source_target_pairs={{0,3},{1,0},{2,1},{3,2},{4,7},{5,4},{6,5},{7,6},{8,11},{9,8},{10,9... | collective-permute-start | bytes 196616 | tf_op jit(solution)/shard_map/ppermute | solution.py:225
  43.3 6.9 %collective-permute-start.1 = (bf16[8,8,512]{2,1,0:T(8,128)(2,1)S(1)}, bf16[8,8,512]{2,1,0:T(8,128)(2,1)S(1)}, u32[]{:S(2)}, u32[]{:S(2)}) collective-permute-start(bf16[8,8,512]{2,1,0:T(8,128)(2,1)S(1)} %all-to-all-done.1.b0), channel_id=1, source_target_pairs={{0,2},{1,3},{2,0},{3,1},{4,6},{5,7},{6,4},{7,5},{8,10},{9,11},{10,... | collective-permute-start | bytes 196616 | tf_op jit(solution)/shard_map/ppermute | solution.py:225
  45.2 6.9 %collective-permute-start = (bf16[8,8,512]{2,1,0:T(8,128)(2,1)S(1)}, bf16[8,8,512]{2,1,0:T(8,128)(2,1)S(1)}, u32[]{:S(2)}, u32[]{:S(2)}) collective-permute-start(bf16[8,8,512]{2,1,0:T(8,128)(2,1)S(1)} %all-to-all-done.1.b0), channel_id=1, source_target_pairs={{0,1},{1,2},{2,3},{3,0},{4,5},{5,6},{6,7},{7,4},{8,9},{9,10},{10,1... | collective-permute-start | bytes 196616 | tf_op jit(solution)/shard_map/ppermute | solution.py:225

commit v3 on v2

--- a/solution.py
+++ b/solution.py
@@ -9,6 +9,9 @@
 STEP = 100
 adapter_scale = 0.5
 learn_rate = 0.05
+DP_ORDER = [(4 + i) % 8 for i in range(8)]
+PLANE_FIRST = 56
+PLANE_ORDER = [(PLANE_FIRST + i) % 64 for i in range(64)]
 SMALL = pltpu.CompilerParams(vmem_limit_bytes=16 * 1024 * 1024)
 
 
@@ -41,12 +44,12 @@
     for l in range(2):
         for j in range(3):
             for d in range(8):
-                scr[d, 4 * l : 4 * l + 4, 128 * j : 128 * j + 128] = ga_ref[
+                scr[DP_ORDER.index(d), 4 * l : 4 * l + 4, 128 * j : 128 * j + 128] = ga_ref[
                     l, pl.ds(12 * d + j, 4, stride=3), :
                 ]
         for d in range(8):
-            scr[d, 4 * l : 4 * l + 2, 384:896] = gb_ref[0, l, 2 * d : 2 * d + 2, 0:512]
-            scr[d, 4 * l + 2 : 4 * l + 4, 384:768] = gb_ref[0, l, 2 * d : 2 * d + 2, 512:896]
+            scr[DP_ORDER.index(d), 4 * l : 4 * l + 2, 384:896] = gb_ref[0, l, 2 * d : 2 * d + 2, 0:512]
+            scr[DP_ORDER.index(d), 4 * l + 2 : 4 * l + 4, 384:768] = gb_ref[0, l, 2 * d : 2 * d + 2, 512:896]
     m_ref[...] = scr[...].astype(jnp.bfloat16)
 
 
@@ -93,67 +96,59 @@
         sb_ref[i] = block
 
 
-def merge_kernel(ra_ref, b0, b1, b2, b3, codes_ref, scale_ref, *refs):
-    state_in, out_hbm, peak_ref, state_out = refs[:6], refs[6], refs[7], refs[8:14]
-    out_ref, asc, bsc, sems = refs[14:]
+def prepare_kernel(ra_ref, codes_ref, scale_ref, left_ref, frozen_ref, asc, wide):
+    cut = 64 - PLANE_FIRST
+    asc[0 : 8 * PLANE_FIRST] = ra_ref[cut:64].astype(jnp.float32).reshape(8 * PLANE_FIRST, 128)
+    asc[8 * PLANE_FIRST : 512] = ra_ref[0:cut].astype(jnp.float32).reshape(8 * cut, 128)
+    me = lax.axis_index("tp")
+    wide[...] = jnp.zeros((12, 256, 128), jnp.float32)
+    for i in range(4):
+        peer = lax.rem(me + 4 - i, 4)
+        for l in range(2):
+            for j in range(3):
+                for k in range(2):
+                    rows = asc[pl.ds(128 * peer + 8 * k + 3 * l + j, 8, stride=16), :]
+                    rows = adapter_scale * jnp.concatenate([rows[4:8], rows[0:4]], axis=0)
+                    for h in range(2):
+                        wide[6 * l + 3 * h + j, pl.ds(64 * i + 4 * l + 2 * h + k, 8, stride=8), :] = rows
+    for n in range(12):
+        left_ref[n] = wide[n].T.astype(jnp.bfloat16)
+    for l in range(2):
+        for j in range(3):
+            rows = slice(QBLK * j, QBLK * j + QBLK)
+            for block in range(7):
+                cols = slice(QBLK * block, QBLK * block + QBLK)
+                scale = scale_ref[j, l : l + 1, block : block + 1]
+                frozen_ref[l, rows, cols] = codes_ref[l, rows, cols].astype(jnp.float32) * scale
+
+
+def merge_kernel(left_ref, b0, b1, b2, b3, frozen_ref, *refs):
+    state_in, out_hbm, peak_hbm, state_out = refs[:6], refs[6], refs[7], refs[8:14]
+    out_ref, peak_ref, sems = refs[14:]
     states = [
         pltpu.make_async_copy(a, b, sems.at[6 + i])
         for i, (a, b) in enumerate(zip(state_in, state_out))
     ]
     for copy in states:
         copy.start()
-    asc[...] = ra_ref[...].astype(jnp.float32).reshape(512, 128)
-    for i, b_ref in enumerate((b0, b1, b2, b3)):
-        for q in range(4):
-            bsc[i, q] = b_ref[:, :, 128 * q : 128 * q + 128].astype(jnp.float32).reshape(64, 128)
-    me = lax.axis_index("tp")
-    peers = [lax.rem(me + 4 - i, 4) for i in range(4)]
     lane = lax.broadcasted_iota(jnp.int32, (1, 7), 1)
+    right = jnp.concatenate([b_ref[...].reshape(64, 512) for b_ref in (b0, b1, b2, b3)], axis=0)
     copies = []
     for l in range(2):
-        halves = []
-        for h, width in enumerate((512, 384)):
-            row = 4 * l + 2 * h
-            tiles = [
-                jnp.concatenate(
-                    [
-                        bsc[i, q, pl.ds(row + k, 8, stride=8), :]
-                        for i in range(4)
-                        for k in range(2)
-                    ],
-                    axis=0,
-                )
-                for q in range(width // QBLK)
-            ]
-            halves.append(jnp.concatenate(tiles, axis=1).astype(jnp.bfloat16))
         for j in range(3):
             row = 3 * l + j
-            left = jnp.concatenate(
-                [
-                    asc[pl.ds(128 * peers[i] + 8 * k + row, 8, stride=16), :]
-                    for i in range(4)
-                    for k in range(2)
-                ],
-                axis=0,
-            )
-            left = (adapter_scale * left).astype(jnp.bfloat16)
             peaks = jnp.zeros((1, 7), jnp.float32)
             rows = slice(QBLK * j, QBLK * j + QBLK)
             for h, width in enumerate((512, 384)):
-                product = lax.dot_general(
-                    left,
-                    halves[h],
-                    (((0,), (0,)), ((), ())),
+                product = jnp.dot(
+                    left_ref[6 * l + 3 * h + j],
+                    right[:, 0:width],
                     preferred_element_type=jnp.float32,
                 )
                 for c in range(width // QBLK):
                     block = 4 * h + c
                     cols = slice(QBLK * block, QBLK * block + QBLK)
-                    scale = scale_ref[j, l : l + 1, block : block + 1]
-                    merged = (
-                        codes_ref[l, rows, cols].astype(jnp.float32) * scale
-                        + product[:, QBLK * c : QBLK * c + QBLK]
-                    )
+                    merged = frozen_ref[l, rows, cols] + product[:, QBLK * c : QBLK * c + QBLK]
                     peak = (
                         jnp.max(
                             jnp.max(jnp.abs(merged), axis=0, keepdims=True), axis=1, keepdims=True
@@ -169,6 +164,8 @@
                 )
             )
             copies[-1].start()
+    copies.append(pltpu.make_async_copy(peak_ref, peak_hbm, sems.at[12]))
+    copies[-1].start()
     for copy in states + copies:
         copy.wait()
 
@@ -197,7 +194,9 @@
         cost_estimate=pl.CostEstimate(flops=10**9, bytes_accessed=400000, transcendentals=0),
         name="pack",
     )(ga.reshape(2, 96, 128), gb, first)
-    received = lax.all_to_all(messages, "dp", 0, 0, tiled=True)
+    received = lax.all_to_all(
+        messages, "dp", 0, 0, tiled=True, axis_index_groups=[DP_ORDER]
+    )
     pb, mb, vb, send_b = pl.pallas_call(
         adam_b_kernel,
         out_shape=b_state + [sds((8, 8, 512), bf16)],
@@ -208,7 +207,7 @@
         cost_estimate=pl.CostEstimate(flops=100000, bytes_accessed=400000, transcendentals=3584),
         name="adam_b",
     )(received, pb, mb, vb)
-    all_b = [lax.all_to_all(send_b, "dp", 0, 0, tiled=True)]
+    all_b = [lax.all_to_all(send_b, "dp", 0, 0, tiled=True, axis_index_groups=[DP_ORDER])]
     pa, ma, va, send_a = pl.pallas_call(
         adam_a_kernel,
         out_shape=a_state + [sds((64, 8, 128), bf16)],
@@ -220,23 +219,34 @@
         name="adam_a",
     )(received, pa, ma, va, send_b)
     all_b[0], send_a = lax.optimization_barrier((all_b[0], send_a))
-    all_a = lax.all_to_all(send_a, ("roll", "tp"), 0, 0, tiled=True)
+    all_a = lax.all_to_all(
+        send_a, ("roll", "tp"), 0, 0, tiled=True, axis_index_groups=[PLANE_ORDER]
+    )
     for shift in range(1, 4):
         all_b.append(lax.ppermute(all_b[0], "tp", [(i, (i + shift) % 4) for i in range(4)]))
+    left, frozen = pl.pallas_call(
+        prepare_kernel,
+        out_shape=[sds((12, 128, 256), bf16), sds((2, 384, 896), f32)],
+        in_specs=vmem(3),
+        out_specs=vmem(2),
+        scratch_shapes=[pltpu.VMEM((512, 128), f32), pltpu.VMEM((12, 256, 128), f32)],
+        compiler_params=SMALL,
+        cost_estimate=pl.CostEstimate(flops=10**6, bytes_accessed=4000000, transcendentals=0),
+        name="prepare",
+    )(all_a, codes, scales.transpose(1, 0, 2))
     out, peaks, pa, ma, va, pb, mb, vb = pl.pallas_call(
         merge_kernel,
         out_shape=[sds((2, 384, 896), bf16), sds((3, 2, 7), f32)] + a_state + b_state,
-        in_specs=vmem(13),
-        out_specs=hbm(1) + vmem(1) + hbm(6),
+        in_specs=vmem(12),
+        out_specs=hbm(8),
         scratch_shapes=[
             pltpu.VMEM((2, 384, 896), bf16),
-            pltpu.VMEM((512, 128), f32),
-            pltpu.VMEM((4, 4, 64, 128), f32),
-            pltpu.SemaphoreType.DMA((12,)),
+            pltpu.VMEM((3, 2, 7), f32),
+            pltpu.SemaphoreType.DMA((13,)),
         ],
         compiler_params=SMALL,
         name="merge",
-    )(all_a, *all_b, codes, scales.transpose(1, 0, 2), pa, ma, va, pb, mb, vb)
+    )(left, *all_b, frozen, pa, ma, va, pb, mb, vb)
     return (
         out,
         peaks.transpose(1, 0, 2),

time: 55.3 us -> 53.6 us (0.969)
  the two profiles are of different devices: /device:TPU:1 before, /device:TPU:4 now
where the time goes in v3:
time: 53.6 us; the launch traced here: 53.2 us
  starting transfers between devices  25.6 us (48%)
  blocking collectives  13 us (24%)
  waiting for transfers between devices  8.18 us (15%)
  Pallas kernels  4.64 us (9%)
  local copies, waits for them, and re-layouts  0.96 us (2%)
  between operations  0.78 us (1%)
    all_to_all x1, blocking collectives, shards(): lax.all_to_all(messages, 'dp', 0, 0, tiled=True, axis_index_groups=[DP_OR...  13 us
    all_to_all x1, starting transfers between devices, shards(): lax.all_to_all(send_a, ('roll', 'tp'), 0, 0, tiled=True, axis_index_group...  12.1 us
    ppermute x3, starting transfers between devices, shards(): lax.ppermute(all_b[0], 'tp', [(i, (i + shift) % 4) for i in range(4)])  10.1 us
    all_to_all x1, waiting for transfers between devices, shards(): lax.all_to_all(send_b, 'dp', 0, 0, tiled=True, axis_index_groups=[DP_ORDER])  3.93 us
    ppermute x3, waiting for transfers between devices, shards(): lax.ppermute(all_b[0], 'tp', [(i, (i + shift) % 4) for i in range(4)])  3.68 us
    all_to_all x1, starting transfers between devices, shards(): lax.all_to_all(send_b, 'dp', 0, 0, tiled=True, axis_index_groups=[DP_ORDER])  3.35 us
    pallas_call x1, Pallas kernels, shards(): pl.pallas_call(merge_kernel, out_shape=[sds((2, 384, 896), bf16), sds((3,...  1.65 us
    pallas_call x1, Pallas kernels, shards(): pl.pallas_call(adam_a_kernel, out_shape=a_state + [sds((64, 8, 128), bf16...  1.58 us
  transfers between devices with their start and end apart: 5, of which 4 were waited for; matrix products, arithmetic and copies ran while one was open for 0% of the time, Pallas kernels for 4%

profile of v3, /device:TPU:4, one launch (start us, length us, event | category | flops | bytes accessed | tf_op | source)
XLA Modules:
  0.0 53.2 jit_solution(6376910370177906778)
XLA Ops:
  0.6 0.0 copy-start.8
  0.6 0.0 copy-start.9
  0.7 0.9 %copy-done.8 = f32[1,2,16,896]{3,2,1,0:T(8,128)S(1)} copy-done((f32[1,2,16,896]{3,2,1,0:T(8,128)S(1)}, f32[1,2,16,896]{3,2,1,0:T(8,128)}, u32[]{:S(2)}) %copy-start.8) | copy-done | bytes 114712
  1.5 0.1 copy-done.9
  1.6 0.0 copy-start.1
  1.6 0.0 copy-start.2
  1.6 0.0 copy-start.3
  1.6 0.0 copy-start.4
  1.6 0.0 copy-start.5
  1.6 0.0 copy-start.6
  1.6 0.0 copy-start
  1.6 0.0 copy-start.7
  1.6 0.1 pack.1
  1.7 13.0 %all_to_all.15.r_ref = bf16[8,8,896]{2,1,0:T(8,128)(2,1)S(1)} all-to-all(bf16[8,8,896]{2,1,0:T(8,128)(2,1)S(1)} %pack.1), channel_id=1, replica_groups={{256,320,384,448,0,64,128,192},{257,321,385,449,1,65,129,193},{258,322,..., dimensions={0} | all-to-all | bytes 229376 | tf_op jit(solution)/shard_map/all_to_all | solution.py:197
  14.8 0.0 copy-done.1
  14.8 0.0 copy-done.2
  14.8 0.0 copy-done.3
  14.8 0.7 %adam_b.1 = (f32[2,2,896]{2,1,0:T(2,128)S(1)}, f32[2,2,896]{2,1,0:T(2,128)S(1)}, f32[2,2,896]{2,1,0:T(2,128)S(1)}, bf16[8,8,512]{2,1,0:T(8,128)(2,1)}) custom-call(bf16[8,8,896]{2,1,0:T(8,128)(2,1)S(1)} %all_to_all.15.r_ref, f32[2,2,896]{2,1,0:T(2,128)S(1)} %copy-done.1, f32[2,2,896]{2,1,0:T(2,128)S(1)} %copy-done.2, f32[2,2,896]{2,1,0:T(2,128)S(1)} %copy-done.3), custom_call_target="tpu_custom_call" | custom-call | flops 100000 | bytes 400000 | tf_op jit(solution)/shard_map/adam_b/pallas_call | solution.py:200
  15.5 3.3 %all-to-all-start.1 = ((bf16[8,8,512]{2,1,0:T(8,128)(2,1)}), bf16[8,8,512]{2,1,0:T(8,128)(2,1)S(1)}, u32[]{:S(2)}, u32[]{:S(2)}) async-start(bf16[8,8,512]{2,1,0:T(8,128)(2,1)} %get-tuple-element.28.order_ref), calls=%async_computation.1 | async-start | bytes 131072 | tf_op jit(solution)/shard_map/all_to_all | solution.py:210
  18.8 0.0 copy-done.4
  18.8 0.0 copy-done.5
  18.8 0.0 copy-done.6
  18.8 1.6 %adam_a.1 = (f32[24,128]{1,0:T(8,128)S(1)}, f32[24,128]{1,0:T(8,128)S(1)}, f32[24,128]{1,0:T(8,128)S(1)}, bf16[64,8,128]{2,1,0:T(8,128)(2,1)}) custom-call(bf16[8,8,896]{2,1,0:T(8,128)(2,1)S(1)} %all_to_all.15.r_ref, f32[24,128]{1,0:T(8,128)S(1)} %bitcast.9, f32[24,128]{1,0:T(8,128)S(1)} %bitcast.10, f32[24,128]{1,0:T(8,128)S(1)} %bitcast.11, ...), custom_call_target="tpu_custom_call" | custom-call | flops 100000 | bytes 200000 | tf_op jit(solution)/shard_map/adam_a/pallas_call | solution.py:211
  20.4 3.9 %all-to-all-done.1.b0 = bf16[8,8,512]{2,1,0:T(8,128)(2,1)S(1)} async-done(((bf16[8,8,512]{2,1,0:T(8,128)(2,1)}), bf16[8,8,512]{2,1,0:T(8,128)(2,1)S(1)}, u32[]{:S(2)}, u32[]{:S(2)}) %all-to-all-start.1) | async-done | bytes 65568 | tf_op jit(solution)/shard_map/all_to_all | solution.py:210
  24.4 12.1 %all-to-all-start.2 = ((bf16[64,8,128]{2,1,0:T(8,128)(2,1)}), bf16[64,8,128]{2,1,0:T(8,128)(2,1)S(1)}, u32[]{:S(2)}, u32[]{:S(2)}) async-start(bf16[64,8,128]{2,1,0:T(8,128)(2,1)} %get-tuple-element.30), calls=%async_computation.2 | async-start | bytes 262144 | tf_op jit(solution)/shard_map/all_to_all | solution.py:222
  36.5 5.2 %collective-permute-start.2 = (bf16[8,8,512]{2,1,0:T(8,128)(2,1)S(1)}, bf16[8,8,512]{2,1,0:T(8,128)(2,1)S(1)}, u32[]{:S(2)}, u32[]{:S(2)}) collective-permute-start(bf16[8,8,512]{2,1,0:T(8,128)(2,1)S(1)} %all-to-all-done.1.b0), channel_id=1, source_target_pairs={{0,3},{1,0},{2,1},{3,2},{4,7},{5,4},{6,5},{7,6},{8,11},{9,8},{10,9... | collective-permute-start | bytes 196616 | tf_op jit(solution)/shard_map/ppermute | solution.py:226
  41.7 1.9 %collective-permute-start.1 = (bf16[8,8,512]{2,1,0:T(8,128)(2,1)S(1)}, bf16[8,8,512]{2,1,0:T(8,128)(2,1)S(1)}, u32[]{:S(2)}, u32[]{:S(2)}) collective-permute-start(bf16[8,8,512]{2,1,0:T(8,128)(2,1)S(1)} %all-to-all-done.1.b0), channel_id=1, source_target_pairs={{0,2},{1,3},{2,0},{3,1},{4,6},{5,7},{6,4},{7,5},{8,10},{9,11},{10,... | collective-permute-start | bytes 196616 | tf_op jit(solution)/shard_map/ppermute | solution.py:226
  43.6 3.0 %collective-permute-start = (bf16[8,8,512]{2,1,0:T(8,128)(2,1)S(1)}, bf16[8,8,512]{2,1,0:T(8,128)(2,1)S(1)}, u32[]{:S(2)}, u32[]{:S(2)}) collective-permute-start(bf16[8,8,512]{2,1,0:T(8,128)(2,1)S(1)} %all-to-all-done.1.b0), channel_id=1, source_target_pairs={{0,1},{1,2},{2,3},{3,0},{4,5},{5,6},{6,7},{7,4},{8,9},{9,10},{10,1... | collective-permute-start | bytes 196616 | tf_op jit(solution)/shard_map/ppermute | solution.py:226
  46.6 0.6 %all-to-all-done.2.ra_ref = bf16[64,8,128]{2,1,0:T(8,128)(2,1)S(1)} async-done(((bf16[64,8,128]{2,1,0:T(8,128)(2,1)}), bf16[64,8,128]{2,1,0:T(8,128)(2,1)S(1)}, u32[]{:S(2)}, u32[]{:S(2)}) %all-to-all-start.2) | async-done | bytes 131104 | tf_op jit(solution)/shard_map/all_to_all | solution.py:222
  47.2 0.0 copy-done
  47.2 0.0 copy-done.7
  47.2 0.7 %prepare.1 = (bf16[12,128,256]{2,1,0:T(8,128)(2,1)S(1)}, f32[2,384,896]{2,1,0:T(8,128)S(1)}) custom-call(bf16[64,8,128]{2,1,0:T(8,128)(2,1)S(1)} %all-to-all-done.2.ra_ref, bf16[2,384,896]{2,1,0:T(8,128)(2,1)S(1)} %copy-done, f32[3,2,7]{2,1,0:T(2,128)S(1)} %bitcast.12), custom_call_target="tpu_custom_call" | custom-call | flops 1000000 | bytes 4000000 | tf_op jit(solution)/shard_map/prepare/pallas_call | solution.py:227
  47.9 0.0 collective-permute-done.2.b3
  47.9 0.9 %collective-permute-done.1.b2 = bf16[8,8,512]{2,1,0:T(8,128)(2,1)S(1)} collective-permute-done((bf16[8,8,512]{2,1,0:T(8,128)(2,1)S(1)}, bf16[8,8,512]{2,1,0:T(8,128)(2,1)S(1)}, u32[]{:S(2)}, u32[]{:S(2)}) %collective-permute-start.1) | collective-permute-done | bytes 65568 | tf_op jit(solution)/shard_map/ppermute | solution.py:226
  48.7 2.8 %collective-permute-done.b1 = bf16[8,8,512]{2,1,0:T(8,128)(2,1)S(1)} collective-permute-done((bf16[8,8,512]{2,1,0:T(8,128)(2,1)S(1)}, bf16[8,8,512]{2,1,0:T(8,128)(2,1)S(1)}, u32[]{:S(2)}, u32[]{:S(2)}) %collective-permute-start) | collective-permute-done | bytes 65568 | tf_op jit(solution)/shard_map/ppermute | solution.py:226
  51.6 1.6 %merge.1 = (bf16[2,384,896]{2,1,0:T(8,128)(2,1)}, f32[3,2,7]{2,1,0:T(2,128)}, f32[24,128]{1,0:T(8,128)}, f32[24,128]{1,0:T(8,128)}, f32[24,128]{1,0:T(8,128)}, /...) custom-call(bf16[12,128,256]{2,1,0:T(8,128)(2,1)S(1)} %get-tuple-element.31.left_ref, ...), custom_call_target="tpu_custom_call" | custom-call | tf_op jit(solution)/shard_map/merge/pallas_call | solution.py:237
  (1 shorter events, 0.0 us)
Async XLA Ops:
  0.6 0.9 %copy-start.8 = (f32[1,2,16,896]{3,2,1,0:T(8,128)S(1)}, f32[1,2,16,896]{3,2,1,0:T(8,128)}, u32[]{:S(2)}) copy-start(f32[1,2,16,896]{3,2,1,0:T(8,128)} %gb_ref.1) | copy-start | bytes 344068
  0.6 0.9 %copy-start.9 = (f32[1,2,1,12288]{3,2,1,0:T(1,128)S(1)}, f32[1,2,1,12288]{3,2,1,0:T(1,128)}, u32[]{:S(2)}) copy-start(f32[1,2,1,12288]{3,2,1,0:T(1,128)} %param.10) | copy-start | bytes 294916
  1.6 13.2 %copy-start.1 = (f32[2,2,896]{2,1,0:T(2,128)S(1)}, f32[2,2,896]{2,1,0:T(2,128)}, u32[]{:S(2)}) copy-start(f32[2,2,896]{2,1,0:T(2,128)} %pb.1) | copy-start | bytes 43012
  1.6 13.2 %copy-start.2 = (f32[2,2,896]{2,1,0:T(2,128)S(1)}, f32[2,2,896]{2,1,0:T(2,128)}, u32[]{:S(2)}) copy-start(f32[2,2,896]{2,1,0:T(2,128)} %mb.1) | copy-start | bytes 43012
  1.6 13.2 %copy-start.3 = (f32[2,2,896]{2,1,0:T(2,128)S(1)}, f32[2,2,896]{2,1,0:T(2,128)}, u32[]{:S(2)}) copy-start(f32[2,2,896]{2,1,0:T(2,128)} %vb.1) | copy-start | bytes 43012
  1.6 17.2 %copy-start.4 = (f32[2,1,1536]{2,1,0:T(1,128)S(1)}, f32[2,1,1536]{2,1,0:T(1,128)}, u32[]{:S(2)}) copy-start(f32[2,1,1536]{2,1,0:T(1,128)} %param.12) | copy-start | bytes 36868
  1.6 17.2 %copy-start.5 = (f32[2,1,1536]{2,1,0:T(1,128)S(1)}, f32[2,1,1536]{2,1,0:T(1,128)}, u32[]{:S(2)}) copy-start(f32[2,1,1536]{2,1,0:T(1,128)} %param.13) | copy-start | bytes 36868
  1.6 17.2 %copy-start.6 = (f32[2,1,1536]{2,1,0:T(1,128)S(1)}, f32[2,1,1536]{2,1,0:T(1,128)}, u32[]{:S(2)}) copy-start(f32[2,1,1536]{2,1,0:T(1,128)} %param.14) | copy-start | bytes 36868
  1.6 45.6 %copy-start = (bf16[2,384,896]{2,1,0:T(8,128)(2,1)S(1)}, bf16[2,384,896]{2,1,0:T(8,128)(2,1)}, u32[]{:S(2)}) copy-start(bf16[2,384,896]{2,1,0:T(8,128)(2,1)} %codes_ref.1) | copy-start | bytes 4128772
  1.6 45.6 %copy-start.7 = (f32[2,3,7]{2,0,1:T(2,128)S(1)}, f32[2,3,7]{2,0,1:T(2,128)}, u32[]{:S(2)}) copy-start(f32[2,3,7]{2,0,1:T(2,128)} %param.19) | copy-start | bytes 508
  15.5 8.9 %all-to-all-start.1 = ((bf16[8,8,512]{2,1,0:T(8,128)(2,1)}), bf16[8,8,512]{2,1,0:T(8,128)(2,1)S(1)}, u32[]{:S(2)}, u32[]{:S(2)}) async-start(bf16[8,8,512]{2,1,0:T(8,128)(2,1)} %get-tuple-element.28.order_ref), calls=%async_computation.1 | async-start | bytes 131072 | tf_op jit(solution)/shard_map/all_to_all | solution.py:210
  24.4 22.8 %all-to-all-start.2 = ((bf16[64,8,128]{2,1,0:T(8,128)(2,1)}), bf16[64,8,128]{2,1,0:T(8,128)(2,1)S(1)}, u32[]{:S(2)}, u32[]{:S(2)}) async-start(bf16[64,8,128]{2,1,0:T(8,128)(2,1)} %get-tuple-element.30), calls=%async_computation.2 | async-start | bytes 262144 | tf_op jit(solution)/shard_map/all_to_all | solution.py:222
  36.5 11.4 %collective-permute-start.2 = (bf16[8,8,512]{2,1,0:T(8,128)(2,1)S(1)}, bf16[8,8,512]{2,1,0:T(8,128)(2,1)S(1)}, u32[]{:S(2)}, u32[]{:S(2)}) collective-permute-start(bf16[8,8,512]{2,1,0:T(8,128)(2,1)S(1)} %all-to-all-done.1.b0), channel_id=1, source_target_pairs={{0,3},{1,0},{2,1},{3,2},{4,7},{5,4},{6,5},{7,6},{8,11},{9,8},{10,9... | collective-permute-start | bytes 196616 | tf_op jit(solution)/shard_map/ppermute | solution.py:226
  41.7 7.1 %collective-permute-start.1 = (bf16[8,8,512]{2,1,0:T(8,128)(2,1)S(1)}, bf16[8,8,512]{2,1,0:T(8,128)(2,1)S(1)}, u32[]{:S(2)}, u32[]{:S(2)}) collective-permute-start(bf16[8,8,512]{2,1,0:T(8,128)(2,1)S(1)} %all-to-all-done.1.b0), channel_id=1, source_target_pairs={{0,2},{1,3},{2,0},{3,1},{4,6},{5,7},{6,4},{7,5},{8,10},{9,11},{10,... | collective-permute-start | bytes 196616 | tf_op jit(solution)/shard_map/ppermute | solution.py:226
  43.6 8.0 %collective-permute-start = (bf16[8,8,512]{2,1,0:T(8,128)(2,1)S(1)}, bf16[8,8,512]{2,1,0:T(8,128)(2,1)S(1)}, u32[]{:S(2)}, u32[]{:S(2)}) collective-permute-start(bf16[8,8,512]{2,1,0:T(8,128)(2,1)S(1)} %all-to-all-done.1.b0), channel_id=1, source_target_pairs={{0,1},{1,2},{2,3},{3,0},{4,5},{5,6},{6,7},{7,4},{8,9},{9,10},{10,1... | collective-permute-start | bytes 196616 | tf_op jit(solution)/shard_map/ppermute | solution.py:226

commit v4 on v3

--- a/solution.py
+++ b/solution.py
@@ -103,7 +103,7 @@
     me = lax.axis_index("tp")
     wide[...] = jnp.zeros((12, 256, 128), jnp.float32)
     for i in range(4):
-        peer = lax.rem(me + 4 - i, 4)
+        peer = lax.bitwise_xor(me, i)
         for l in range(2):
             for j in range(3):
                 for k in range(2):
@@ -222,8 +222,8 @@
     all_a = lax.all_to_all(
         send_a, ("roll", "tp"), 0, 0, tiled=True, axis_index_groups=[PLANE_ORDER]
     )
-    for shift in range(1, 4):
-        all_b.append(lax.ppermute(all_b[0], "tp", [(i, (i + shift) % 4) for i in range(4)]))
+    for i in range(1, 4):
+        all_b.append(lax.ppermute(all_b[0], "tp", [(t, t ^ i) for t in range(4)]))
     left, frozen = pl.pallas_call(
         prepare_kernel,
         out_shape=[sds((12, 128, 256), bf16), sds((2, 384, 896), f32)],

time: 53.6 us -> 52.2 us (0.974)
  the two profiles are of different devices: /device:TPU:4 before, /device:TPU:20 now
where the time goes in v4:
time: 52.2 us; the launch traced here: 51.7 us
  starting transfers between devices  29.4 us (56%)
  blocking collectives  8.47 us (16%)
  waiting for transfers between devices  7.45 us (14%)
  Pallas kernels  4.65 us (9%)
  local copies, waits for them, and re-layouts  0.96 us (2%)
  between operations  0.81 us (2%)
    all_to_all x1, starting transfers between devices, shards(): lax.all_to_all(send_a, ('roll', 'tp'), 0, 0, tiled=True, axis_index_group...  16.5 us
    ppermute x3, starting transfers between devices, shards(): all_b.append(lax.ppermute(all_b[0], 'tp', [(t, t ^ i) for t in range(4)]))  9.56 us
    all_to_all x1, blocking collectives, shards(): lax.all_to_all(messages, 'dp', 0, 0, tiled=True, axis_index_groups=[DP_OR...  8.47 us
    all_to_all x1, waiting for transfers between devices, shards(): lax.all_to_all(send_b, 'dp', 0, 0, tiled=True, axis_index_groups=[DP_ORDER])  3.93 us
    ppermute x3, waiting for transfers between devices, shards(): all_b.append(lax.ppermute(all_b[0], 'tp', [(t, t ^ i) for t in range(4)]))  3.51 us
    all_to_all x1, starting transfers between devices, shards(): lax.all_to_all(send_b, 'dp', 0, 0, tiled=True, axis_index_groups=[DP_ORDER])  3.35 us
    pallas_call x1, Pallas kernels, shards(): pl.pallas_call(merge_kernel, out_shape=[sds((2, 384, 896), bf16), sds((3,...  1.64 us
    pallas_call x1, Pallas kernels, shards(): pl.pallas_call(adam_a_kernel, out_shape=a_state + [sds((64, 8, 128), bf16...  1.58 us
  transfers between devices with their start and end apart: 5, of which 2 were waited for; matrix products, arithmetic and copies ran while one was open for 0% of the time, Pallas kernels for 4%

profile of v4, /device:TPU:20, one launch (start us, length us, event | category | flops | bytes accessed | tf_op | source)
XLA Modules:
  0.0 51.7 jit_solution(8098102169753926018)
XLA Ops:
  0.6 0.0 copy-start.8
  0.6 0.0 copy-start.9
  0.7 0.9 %copy-done.8 = f32[1,2,16,896]{3,2,1,0:T(8,128)S(1)} copy-done((f32[1,2,16,896]{3,2,1,0:T(8,128)S(1)}, f32[1,2,16,896]{3,2,1,0:T(8,128)}, u32[]{:S(2)}) %copy-start.8) | copy-done | bytes 114712
  1.5 0.1 copy-done.9
  1.6 0.0 copy-start.1
  1.6 0.0 copy-start.2
  1.6 0.0 copy-start.3
  1.6 0.0 copy-start.4
  1.6 0.0 copy-start.5
  1.6 0.0 copy-start.6
  1.6 0.0 copy-start
  1.6 0.0 copy-start.7
  1.6 0.1 pack.1
  1.7 8.5 %all_to_all.15.r_ref = bf16[8,8,896]{2,1,0:T(8,128)(2,1)S(1)} all-to-all(bf16[8,8,896]{2,1,0:T(8,128)(2,1)S(1)} %pack.1), channel_id=1, replica_groups={{256,320,384,448,0,64,128,192},{257,321,385,449,1,65,129,193},{258,322,..., dimensions={0} | all-to-all | bytes 229376 | tf_op jit(solution)/shard_map/all_to_all | solution.py:197
  10.2 0.0 copy-done.1
  10.2 0.0 copy-done.2
  10.2 0.0 copy-done.3
  10.2 0.7 %adam_b.1 = (f32[2,2,896]{2,1,0:T(2,128)S(1)}, f32[2,2,896]{2,1,0:T(2,128)S(1)}, f32[2,2,896]{2,1,0:T(2,128)S(1)}, bf16[8,8,512]{2,1,0:T(8,128)(2,1)}) custom-call(bf16[8,8,896]{2,1,0:T(8,128)(2,1)S(1)} %all_to_all.15.r_ref, f32[2,2,896]{2,1,0:T(2,128)S(1)} %copy-done.1, f32[2,2,896]{2,1,0:T(2,128)S(1)} %copy-done.2, f32[2,2,896]{2,1,0:T(2,128)S(1)} %copy-done.3), custom_call_target="tpu_custom_call" | custom-call | flops 100000 | bytes 400000 | tf_op jit(solution)/shard_map/adam_b/pallas_call | solution.py:200
  10.9 3.3 %all-to-all-start.1 = ((bf16[8,8,512]{2,1,0:T(8,128)(2,1)}), bf16[8,8,512]{2,1,0:T(8,128)(2,1)S(1)}, u32[]{:S(2)}, u32[]{:S(2)}) async-start(bf16[8,8,512]{2,1,0:T(8,128)(2,1)} %get-tuple-element.28.order_ref), calls=%async_computation.1 | async-start | bytes 131072 | tf_op jit(solution)/shard_map/all_to_all | solution.py:210
  14.2 0.0 copy-done.4
  14.3 0.0 copy-done.5
  14.3 0.0 copy-done.6
  14.3 1.6 %adam_a.1 = (f32[24,128]{1,0:T(8,128)S(1)}, f32[24,128]{1,0:T(8,128)S(1)}, f32[24,128]{1,0:T(8,128)S(1)}, bf16[64,8,128]{2,1,0:T(8,128)(2,1)}) custom-call(bf16[8,8,896]{2,1,0:T(8,128)(2,1)S(1)} %all_to_all.15.r_ref, f32[24,128]{1,0:T(8,128)S(1)} %bitcast.9, f32[24,128]{1,0:T(8,128)S(1)} %bitcast.10, f32[24,128]{1,0:T(8,128)S(1)} %bitcast.11, ...), custom_call_target="tpu_custom_call" | custom-call | flops 100000 | bytes 200000 | tf_op jit(solution)/shard_map/adam_a/pallas_call | solution.py:211
  15.8 3.9 %all-to-all-done.1.b0 = bf16[8,8,512]{2,1,0:T(8,128)(2,1)S(1)} async-done(((bf16[8,8,512]{2,1,0:T(8,128)(2,1)}), bf16[8,8,512]{2,1,0:T(8,128)(2,1)S(1)}, u32[]{:S(2)}, u32[]{:S(2)}) %all-to-all-start.1) | async-done | bytes 65568 | tf_op jit(solution)/shard_map/all_to_all | solution.py:210
  19.8 16.5 %all-to-all-start.2 = ((bf16[64,8,128]{2,1,0:T(8,128)(2,1)}), bf16[64,8,128]{2,1,0:T(8,128)(2,1)S(1)}, u32[]{:S(2)}, u32[]{:S(2)}) async-start(bf16[64,8,128]{2,1,0:T(8,128)(2,1)} %get-tuple-element.30), calls=%async_computation.2 | async-start | bytes 262144 | tf_op jit(solution)/shard_map/all_to_all | solution.py:222
  36.3 2.5 %collective-permute-start.2 = (bf16[8,8,512]{2,1,0:T(8,128)(2,1)S(1)}, bf16[8,8,512]{2,1,0:T(8,128)(2,1)S(1)}, u32[]{:S(2)}, u32[]{:S(2)}) collective-permute-start(bf16[8,8,512]{2,1,0:T(8,128)(2,1)S(1)} %all-to-all-done.1.b0), channel_id=1, source_target_pairs={{0,3},{1,2},{2,1},{3,0},{4,7},{5,6},{6,5},{7,4},{8,11},{9,10},{10,... | collective-permute-start | bytes 196616 | tf_op jit(solution)/shard_map/ppermute | solution.py:226
  38.7 5.2 %collective-permute-start.1 = (bf16[8,8,512]{2,1,0:T(8,128)(2,1)S(1)}, bf16[8,8,512]{2,1,0:T(8,128)(2,1)S(1)}, u32[]{:S(2)}, u32[]{:S(2)}) collective-permute-start(bf16[8,8,512]{2,1,0:T(8,128)(2,1)S(1)} %all-to-all-done.1.b0), channel_id=1, source_target_pairs={{0,2},{1,3},{2,0},{3,1},{4,6},{5,7},{6,4},{7,5},{8,10},{9,11},{10,... | collective-permute-start | bytes 196616 | tf_op jit(solution)/shard_map/ppermute | solution.py:226
  43.9 1.9 %collective-permute-start = (bf16[8,8,512]{2,1,0:T(8,128)(2,1)S(1)}, bf16[8,8,512]{2,1,0:T(8,128)(2,1)S(1)}, u32[]{:S(2)}, u32[]{:S(2)}) collective-permute-start(bf16[8,8,512]{2,1,0:T(8,128)(2,1)S(1)} %all-to-all-done.1.b0), channel_id=1, source_target_pairs={{0,1},{1,0},{2,3},{3,2},{4,5},{5,4},{6,7},{7,6},{8,9},{9,8},{10,11... | collective-permute-start | bytes 196616 | tf_op jit(solution)/shard_map/ppermute | solution.py:226
  45.9 0.0 all-to-all-done.2.ra_ref
  45.9 0.0 copy-done
  45.9 0.0 copy-done.7
  45.9 0.7 %prepare.1 = (bf16[12,128,256]{2,1,0:T(8,128)(2,1)S(1)}, f32[2,384,896]{2,1,0:T(8,128)S(1)}) custom-call(bf16[64,8,128]{2,1,0:T(8,128)(2,1)S(1)} %all-to-all-done.2.ra_ref, bf16[2,384,896]{2,1,0:T(8,128)(2,1)S(1)} %copy-done, f32[3,2,7]{2,1,0:T(2,128)S(1)} %bitcast.12), custom_call_target="tpu_custom_call" | custom-call | flops 1000000 | bytes 4000000 | tf_op jit(solution)/shard_map/prepare/pallas_call | solution.py:227
  46.6 0.0 collective-permute-done.2.b3
  46.6 0.0 collective-permute-done.1.b2
  46.6 3.5 %collective-permute-done.b1 = bf16[8,8,512]{2,1,0:T(8,128)(2,1)S(1)} collective-permute-done((bf16[8,8,512]{2,1,0:T(8,128)(2,1)S(1)}, bf16[8,8,512]{2,1,0:T(8,128)(2,1)S(1)}, u32[]{:S(2)}, u32[]{:S(2)}) %collective-permute-start) | collective-permute-done | bytes 65568 | tf_op jit(solution)/shard_map/ppermute | solution.py:226
  50.1 1.6 %merge.1 = (bf16[2,384,896]{2,1,0:T(8,128)(2,1)}, f32[3,2,7]{2,1,0:T(2,128)}, f32[24,128]{1,0:T(8,128)}, f32[24,128]{1,0:T(8,128)}, f32[24,128]{1,0:T(8,128)}, /...) custom-call(bf16[12,128,256]{2,1,0:T(8,128)(2,1)S(1)} %get-tuple-element.31.left_ref, ...), custom_call_target="tpu_custom_call" | custom-call | tf_op jit(solution)/shard_map/merge/pallas_call | solution.py:237
  (1 shorter events, 0.0 us)
Async XLA Ops:
  0.6 0.9 %copy-start.8 = (f32[1,2,16,896]{3,2,1,0:T(8,128)S(1)}, f32[1,2,16,896]{3,2,1,0:T(8,128)}, u32[]{:S(2)}) copy-start(f32[1,2,16,896]{3,2,1,0:T(8,128)} %gb_ref.1) | copy-start | bytes 344068
  0.6 0.9 %copy-start.9 = (f32[1,2,1,12288]{3,2,1,0:T(1,128)S(1)}, f32[1,2,1,12288]{3,2,1,0:T(1,128)}, u32[]{:S(2)}) copy-start(f32[1,2,1,12288]{3,2,1,0:T(1,128)} %param.10) | copy-start | bytes 294916
  1.6 8.6 %copy-start.1 = (f32[2,2,896]{2,1,0:T(2,128)S(1)}, f32[2,2,896]{2,1,0:T(2,128)}, u32[]{:S(2)}) copy-start(f32[2,2,896]{2,1,0:T(2,128)} %pb.1) | copy-start | bytes 43012
  1.6 8.6 %copy-start.2 = (f32[2,2,896]{2,1,0:T(2,128)S(1)}, f32[2,2,896]{2,1,0:T(2,128)}, u32[]{:S(2)}) copy-start(f32[2,2,896]{2,1,0:T(2,128)} %mb.1) | copy-start | bytes 43012
  1.6 8.6 %copy-start.3 = (f32[2,2,896]{2,1,0:T(2,128)S(1)}, f32[2,2,896]{2,1,0:T(2,128)}, u32[]{:S(2)}) copy-start(f32[2,2,896]{2,1,0:T(2,128)} %vb.1) | copy-start | bytes 43012
  1.6 12.7 %copy-start.4 = (f32[2,1,1536]{2,1,0:T(1,128)S(1)}, f32[2,1,1536]{2,1,0:T(1,128)}, u32[]{:S(2)}) copy-start(f32[2,1,1536]{2,1,0:T(1,128)} %param.12) | copy-start | bytes 36868
  1.6 12.7 %copy-start.5 = (f32[2,1,1536]{2,1,0:T(1,128)S(1)}, f32[2,1,1536]{2,1,0:T(1,128)}, u32[]{:S(2)}) copy-start(f32[2,1,1536]{2,1,0:T(1,128)} %param.13) | copy-start | bytes 36868
  1.6 12.7 %copy-start.6 = (f32[2,1,1536]{2,1,0:T(1,128)S(1)}, f32[2,1,1536]{2,1,0:T(1,128)}, u32[]{:S(2)}) copy-start(f32[2,1,1536]{2,1,0:T(1,128)} %param.14) | copy-start | bytes 36868
  1.6 44.2 %copy-start = (bf16[2,384,896]{2,1,0:T(8,128)(2,1)S(1)}, bf16[2,384,896]{2,1,0:T(8,128)(2,1)}, u32[]{:S(2)}) copy-start(bf16[2,384,896]{2,1,0:T(8,128)(2,1)} %codes_ref.1) | copy-start | bytes 4128772
  1.6 44.2 %copy-start.7 = (f32[2,3,7]{2,0,1:T(2,128)S(1)}, f32[2,3,7]{2,0,1:T(2,128)}, u32[]{:S(2)}) copy-start(f32[2,3,7]{2,0,1:T(2,128)} %param.19) | copy-start | bytes 508
  10.9 8.9 %all-to-all-start.1 = ((bf16[8,8,512]{2,1,0:T(8,128)(2,1)}), bf16[8,8,512]{2,1,0:T(8,128)(2,1)S(1)}, u32[]{:S(2)}, u32[]{:S(2)}) async-start(bf16[8,8,512]{2,1,0:T(8,128)(2,1)} %get-tuple-element.28.order_ref), calls=%async_computation.1 | async-start | bytes 131072 | tf_op jit(solution)/shard_map/all_to_all | solution.py:210
  19.8 26.1 %all-to-all-start.2 = ((bf16[64,8,128]{2,1,0:T(8,128)(2,1)}), bf16[64,8,128]{2,1,0:T(8,128)(2,1)S(1)}, u32[]{:S(2)}, u32[]{:S(2)}) async-start(bf16[64,8,128]{2,1,0:T(8,128)(2,1)} %get-tuple-element.30), calls=%async_computation.2 | async-start | bytes 262144 | tf_op jit(solution)/shard_map/all_to_all | solution.py:222
  36.3 10.3 %collective-permute-start.2 = (bf16[8,8,512]{2,1,0:T(8,128)(2,1)S(1)}, bf16[8,8,512]{2,1,0:T(8,128)(2,1)S(1)}, u32[]{:S(2)}, u32[]{:S(2)}) collective-permute-start(bf16[8,8,512]{2,1,0:T(8,128)(2,1)S(1)} %all-to-all-done.1.b0), channel_id=1, source_target_pairs={{0,3},{1,2},{2,1},{3,0},{4,7},{5,6},{6,5},{7,4},{8,11},{9,10},{10,... | collective-permute-start | bytes 196616 | tf_op jit(solution)/shard_map/ppermute | solution.py:226
  38.7 7.8 %collective-permute-start.1 = (bf16[8,8,512]{2,1,0:T(8,128)(2,1)S(1)}, bf16[8,8,512]{2,1,0:T(8,128)(2,1)S(1)}, u32[]{:S(2)}, u32[]{:S(2)}) collective-permute-start(bf16[8,8,512]{2,1,0:T(8,128)(2,1)S(1)} %all-to-all-done.1.b0), channel_id=1, source_target_pairs={{0,2},{1,3},{2,0},{3,1},{4,6},{5,7},{6,4},{7,5},{8,10},{9,11},{10,... | collective-permute-start | bytes 196616 | tf_op jit(solution)/shard_map/ppermute | solution.py:226
  43.9 6.2 %collective-permute-start = (bf16[8,8,512]{2,1,0:T(8,128)(2,1)S(1)}, bf16[8,8,512]{2,1,0:T(8,128)(2,1)S(1)}, u32[]{:S(2)}, u32[]{:S(2)}) collective-permute-start(bf16[8,8,512]{2,1,0:T(8,128)(2,1)S(1)} %all-to-all-done.1.b0), channel_id=1, source_target_pairs={{0,1},{1,0},{2,3},{3,2},{4,5},{5,4},{6,7},{7,6},{8,9},{9,8},{10,11... | collective-permute-start | bytes 196616 | tf_op jit(solution)/shard_map/ppermute | solution.py:226

commit v5 on v4

--- a/solution.py
+++ b/solution.py
@@ -101,9 +101,11 @@
     asc[0 : 8 * PLANE_FIRST] = ra_ref[cut:64].astype(jnp.float32).reshape(8 * PLANE_FIRST, 128)
     asc[8 * PLANE_FIRST : 512] = ra_ref[0:cut].astype(jnp.float32).reshape(8 * cut, 128)
     me = lax.axis_index("tp")
+    core = lax.rem(lax.axis_index("dp"), 2)
+    steps = (0, 3 - core, 1, 2 + core)
     wide[...] = jnp.zeros((12, 256, 128), jnp.float32)
     for i in range(4):
-        peer = lax.bitwise_xor(me, i)
+        peer = lax.bitwise_xor(me, steps[i])
         for l in range(2):
             for j in range(3):
                 for k in range(2):
@@ -222,8 +224,10 @@
     all_a = lax.all_to_all(
         send_a, ("roll", "tp"), 0, 0, tiled=True, axis_index_groups=[PLANE_ORDER]
     )
-    for i in range(1, 4):
-        all_b.append(lax.ppermute(all_b[0], "tp", [(t, t ^ i) for t in range(4)]))
+    far = [(4 * d + t, 4 * d + (t ^ (3 - d % 2))) for d in range(8) for t in range(4)]
+    all_b.append(lax.ppermute(all_b[0], ("dp", "tp"), far))
+    all_b.append(lax.ppermute(all_b[0], "tp", [(t, t ^ 1) for t in range(4)]))
+    all_b.append(lax.ppermute(all_b[1], "dp", [(d, d ^ 1) for d in range(8)]))
     left, frozen = pl.pallas_call(
         prepare_kernel,
         out_shape=[sds((12, 128, 256), bf16), sds((2, 384, 896), f32)],

time: 52.2 us -> 51.6 us (0.989)
  the two profiles are of different devices: /device:TPU:20 before, /device:TPU:1 now
where the time goes in v5:
time: 51.6 us; the launch traced here: 51.1 us
  starting transfers between devices  29.1 us (56%)
  blocking collectives  14 us (27%)
  Pallas kernels  4.63 us (9%)
  waiting for transfers between devices  1.65 us (3%)
  local copies, waits for them, and re-layouts  0.96 us (2%)
  between operations  0.79 us (2%)
    all_to_all x1, blocking collectives, shards(): lax.all_to_all(messages, 'dp', 0, 0, tiled=True, axis_index_groups=[DP_OR...  14 us
    all_to_all x1, starting transfers between devices, shards(): lax.all_to_all(send_a, ('roll', 'tp'), 0, 0, tiled=True, axis_index_group...  11.6 us
    all_to_all x1, starting transfers between devices, shards(): lax.all_to_all(send_b, 'dp', 0, 0, tiled=True, axis_index_groups=[DP_ORDER])  6.48 us
    ppermute x1, starting transfers between devices, shards(): all_b.append(lax.ppermute(all_b[0], ('dp', 'tp'), far))  3.99 us
    ppermute x1, starting transfers between devices, shards(): all_b.append(lax.ppermute(all_b[1], 'dp', [(d, d ^ 1) for d in range(8)]))  3.98 us
    ppermute x1, starting transfers between devices, shards(): all_b.append(lax.ppermute(all_b[0], 'tp', [(t, t ^ 1) for t in range(4)]))  3.09 us
    pallas_call x1, Pallas kernels, shards(): pl.pallas_call(merge_kernel, out_shape=[sds((2, 384, 896), bf16), sds((3,...  1.65 us
    pallas_call x1, Pallas kernels, shards(): pl.pallas_call(adam_a_kernel, out_shape=a_state + [sds((64, 8, 128), bf16...  1.56 us
  transfers between devices with their start and end apart: 5, of which 3 were waited for; matrix products, arithmetic and copies ran while one was open for 0% of the time, Pallas kernels for 4%

profile of v5, /device:TPU:1, one launch (start us, length us, event | category | flops | bytes accessed | tf_op | source)
XLA Modules:
  0.0 51.1 jit_solution(17882666147994170992)
XLA Ops:
  0.6 0.0 copy-start.8
  0.6 0.0 copy-start.9
  0.7 0.9 %copy-done.8 = f32[1,2,16,896]{3,2,1,0:T(8,128)S(1)} copy-done((f32[1,2,16,896]{3,2,1,0:T(8,128)S(1)}, f32[1,2,16,896]{3,2,1,0:T(8,128)}, u32[]{:S(2)}) %copy-start.8) | copy-done | bytes 114712
  1.5 0.1 copy-done.9
  1.6 0.0 copy-start.1
  1.6 0.0 copy-start.2
  1.6 0.0 copy-start.3
  1.6 0.0 copy-start.4
  1.6 0.0 copy-start.5
  1.6 0.0 copy-start.6
  1.6 0.0 copy-start
  1.6 0.0 copy-start.7
  1.6 0.1 pack.1
  1.7 14.0 %all_to_all.15.r_ref = bf16[8,8,896]{2,1,0:T(8,128)(2,1)S(1)} all-to-all(bf16[8,8,896]{2,1,0:T(8,128)(2,1)S(1)} %pack.1), channel_id=1, replica_groups={{256,320,384,448,0,64,128,192},{257,321,385,449,1,65,129,193},{258,322,..., dimensions={0} | all-to-all | bytes 229376 | tf_op jit(solution)/shard_map/all_to_all | solution.py:199
  15.7 0.0 copy-done.1
  15.7 0.0 copy-done.2
  15.8 0.0 copy-done.3
  15.8 0.7 %adam_b.1 = (f32[2,2,896]{2,1,0:T(2,128)S(1)}, f32[2,2,896]{2,1,0:T(2,128)S(1)}, f32[2,2,896]{2,1,0:T(2,128)S(1)}, bf16[8,8,512]{2,1,0:T(8,128)(2,1)}) custom-call(bf16[8,8,896]{2,1,0:T(8,128)(2,1)S(1)} %all_to_all.15.r_ref, f32[2,2,896]{2,1,0:T(2,128)S(1)} %copy-done.1, f32[2,2,896]{2,1,0:T(2,128)S(1)} %copy-done.2, f32[2,2,896]{2,1,0:T(2,128)S(1)} %copy-done.3), custom_call_target="tpu_custom_call" | custom-call | flops 100000 | bytes 400000 | tf_op jit(solution)/shard_map/adam_b/pallas_call | solution.py:202
  16.4 6.5 %all-to-all-start.1 = ((bf16[8,8,512]{2,1,0:T(8,128)(2,1)}), bf16[8,8,512]{2,1,0:T(8,128)(2,1)S(1)}, u32[]{:S(2)}, u32[]{:S(2)}) async-start(bf16[8,8,512]{2,1,0:T(8,128)(2,1)} %get-tuple-element.28.order_ref), calls=%async_computation.1 | async-start | bytes 131072 | tf_op jit(solution)/shard_map/all_to_all | solution.py:212
  22.9 0.0 copy-done.4
  22.9 0.0 copy-done.5
  22.9 0.0 copy-done.6
  22.9 1.6 %adam_a.1 = (f32[24,128]{1,0:T(8,128)S(1)}, f32[24,128]{1,0:T(8,128)S(1)}, f32[24,128]{1,0:T(8,128)S(1)}, bf16[64,8,128]{2,1,0:T(8,128)(2,1)}) custom-call(bf16[8,8,896]{2,1,0:T(8,128)(2,1)S(1)} %all_to_all.15.r_ref, f32[24,128]{1,0:T(8,128)S(1)} %bitcast.9, f32[24,128]{1,0:T(8,128)S(1)} %bitcast.10, f32[24,128]{1,0:T(8,128)S(1)} %bitcast.11, ...), custom_call_target="tpu_custom_call" | custom-call | flops 100000 | bytes 200000 | tf_op jit(solution)/shard_map/adam_a/pallas_call | solution.py:213
  24.5 0.6 %all-to-all-done.1.b0 = bf16[8,8,512]{2,1,0:T(8,128)(2,1)S(1)} async-done(((bf16[8,8,512]{2,1,0:T(8,128)(2,1)}), bf16[8,8,512]{2,1,0:T(8,128)(2,1)S(1)}, u32[]{:S(2)}, u32[]{:S(2)}) %all-to-all-start.1) | async-done | bytes 65568 | tf_op jit(solution)/shard_map/all_to_all | solution.py:212
  25.1 11.6 %all-to-all-start.2 = ((bf16[64,8,128]{2,1,0:T(8,128)(2,1)}), bf16[64,8,128]{2,1,0:T(8,128)(2,1)S(1)}, u32[]{:S(2)}, u32[]{:S(2)}) async-start(bf16[64,8,128]{2,1,0:T(8,128)(2,1)} %get-tuple-element.30), calls=%async_computation.2 | async-start | bytes 262144 | tf_op jit(solution)/shard_map/all_to_all | solution.py:224
  36.7 4.0 %collective-permute-start = (bf16[8,8,512]{2,1,0:T(8,128)(2,1)S(1)}, bf16[8,8,512]{2,1,0:T(8,128)(2,1)S(1)}, u32[]{:S(2)}, u32[]{:S(2)}) collective-permute-start(bf16[8,8,512]{2,1,0:T(8,128)(2,1)S(1)} %all-to-all-done.1.b0), channel_id=1, source_target_pairs={{0,3},{1,2},{2,1},{3,0},{64,66},{65,67},{66,64},{67,65},{128,131},... | collective-permute-start | bytes 196616 | tf_op jit(solution)/shard_map/ppermute | solution.py:228
  40.7 3.1 %collective-permute-start.1 = (bf16[8,8,512]{2,1,0:T(8,128)(2,1)S(1)}, bf16[8,8,512]{2,1,0:T(8,128)(2,1)S(1)}, u32[]{:S(2)}, u32[]{:S(2)}) collective-permute-start(bf16[8,8,512]{2,1,0:T(8,128)(2,1)S(1)} %all-to-all-done.1.b0), channel_id=1, source_target_pairs={{0,1},{1,0},{2,3},{3,2},{4,5},{5,4},{6,7},{7,6},{8,9},{9,8},{10,11... | collective-permute-start | bytes 196616 | tf_op jit(solution)/shard_map/ppermute | solution.py:229
  43.8 0.8 %collective-permute-done.b1 = bf16[8,8,512]{2,1,0:T(8,128)(2,1)S(1)} collective-permute-done((bf16[8,8,512]{2,1,0:T(8,128)(2,1)S(1)}, bf16[8,8,512]{2,1,0:T(8,128)(2,1)S(1)}, u32[]{:S(2)}, u32[]{:S(2)}) %collective-permute-start) | collective-permute-done | bytes 65568 | tf_op jit(solution)/shard_map/ppermute | solution.py:228
  44.6 4.0 %collective-permute-start.2 = (bf16[8,8,512]{2,1,0:T(8,128)(2,1)S(1)}, bf16[8,8,512]{2,1,0:T(8,128)(2,1)S(1)}, u32[]{:S(2)}, u32[]{:S(2)}) collective-permute-start(bf16[8,8,512]{2,1,0:T(8,128)(2,1)S(1)} %collective-permute-done.b1), channel_id=1, source_target_pairs={{0,64},{64,0},{128,192},{192,128},{256,320},{320,256},{384,448},{4... | collective-permute-start | bytes 196616 | tf_op jit(solution)/shard_map/ppermute | solution.py:230
  48.6 0.0 all-to-all-done.2.ra_ref
  48.6 0.0 copy-done
  48.6 0.0 copy-done.7
  48.6 0.7 %prepare.1 = (bf16[12,128,256]{2,1,0:T(8,128)(2,1)S(1)}, f32[2,384,896]{2,1,0:T(8,128)S(1)}) custom-call(bf16[64,8,128]{2,1,0:T(8,128)(2,1)S(1)} %all-to-all-done.2.ra_ref, bf16[2,384,896]{2,1,0:T(8,128)(2,1)S(1)} %copy-done, f32[3,2,7]{2,1,0:T(2,128)S(1)} %bitcast.12), custom_call_target="tpu_custom_call" | custom-call | flops 1000000 | bytes 4000000 | tf_op jit(solution)/shard_map/prepare/pallas_call | solution.py:231
  49.3 0.0 collective-permute-done.1.b2
  49.3 0.2 collective-permute-done.2.b3
  49.5 1.6 %merge.1 = (bf16[2,384,896]{2,1,0:T(8,128)(2,1)}, f32[3,2,7]{2,1,0:T(2,128)}, f32[24,128]{1,0:T(8,128)}, f32[24,128]{1,0:T(8,128)}, f32[24,128]{1,0:T(8,128)}, /...) custom-call(bf16[12,128,256]{2,1,0:T(8,128)(2,1)S(1)} %get-tuple-element.31.left_ref, ...), custom_call_target="tpu_custom_call" | custom-call | tf_op jit(solution)/shard_map/merge/pallas_call | solution.py:241
  (1 shorter events, 0.0 us)
Async XLA Ops:
  0.6 0.9 %copy-start.8 = (f32[1,2,16,896]{3,2,1,0:T(8,128)S(1)}, f32[1,2,16,896]{3,2,1,0:T(8,128)}, u32[]{:S(2)}) copy-start(f32[1,2,16,896]{3,2,1,0:T(8,128)} %gb_ref.1) | copy-start | bytes 344068
  0.6 0.9 %copy-start.9 = (f32[1,2,1,12288]{3,2,1,0:T(1,128)S(1)}, f32[1,2,1,12288]{3,2,1,0:T(1,128)}, u32[]{:S(2)}) copy-start(f32[1,2,1,12288]{3,2,1,0:T(1,128)} %param.10) | copy-start | bytes 294916
  1.6 14.2 %copy-start.1 = (f32[2,2,896]{2,1,0:T(2,128)S(1)}, f32[2,2,896]{2,1,0:T(2,128)}, u32[]{:S(2)}) copy-start(f32[2,2,896]{2,1,0:T(2,128)} %pb.1) | copy-start | bytes 43012
  1.6 14.2 %copy-start.2 = (f32[2,2,896]{2,1,0:T(2,128)S(1)}, f32[2,2,896]{2,1,0:T(2,128)}, u32[]{:S(2)}) copy-start(f32[2,2,896]{2,1,0:T(2,128)} %mb.1) | copy-start | bytes 43012
  1.6 14.2 %copy-start.3 = (f32[2,2,896]{2,1,0:T(2,128)S(1)}, f32[2,2,896]{2,1,0:T(2,128)}, u32[]{:S(2)}) copy-start(f32[2,2,896]{2,1,0:T(2,128)} %vb.1) | copy-start | bytes 43012
  1.6 21.3 %copy-start.4 = (f32[2,1,1536]{2,1,0:T(1,128)S(1)}, f32[2,1,1536]{2,1,0:T(1,128)}, u32[]{:S(2)}) copy-start(f32[2,1,1536]{2,1,0:T(1,128)} %param.12) | copy-start | bytes 36868
  1.6 21.3 %copy-start.5 = (f32[2,1,1536]{2,1,0:T(1,128)S(1)}, f32[2,1,1536]{2,1,0:T(1,128)}, u32[]{:S(2)}) copy-start(f32[2,1,1536]{2,1,0:T(1,128)} %param.13) | copy-start | bytes 36868
  1.6 21.3 %copy-start.6 = (f32[2,1,1536]{2,1,0:T(1,128)S(1)}, f32[2,1,1536]{2,1,0:T(1,128)}, u32[]{:S(2)}) copy-start(f32[2,1,1536]{2,1,0:T(1,128)} %param.14) | copy-start | bytes 36868
  1.6 47.0 %copy-start = (bf16[2,384,896]{2,1,0:T(8,128)(2,1)S(1)}, bf16[2,384,896]{2,1,0:T(8,128)(2,1)}, u32[]{:S(2)}) copy-start(bf16[2,384,896]{2,1,0:T(8,128)(2,1)} %codes_ref.1) | copy-start | bytes 4128772
  1.6 47.0 %copy-start.7 = (f32[2,3,7]{2,0,1:T(2,128)S(1)}, f32[2,3,7]{2,0,1:T(2,128)}, u32[]{:S(2)}) copy-start(f32[2,3,7]{2,0,1:T(2,128)} %param.19) | copy-start | bytes 508
  16.4 8.7 %all-to-all-start.1 = ((bf16[8,8,512]{2,1,0:T(8,128)(2,1)}), bf16[8,8,512]{2,1,0:T(8,128)(2,1)S(1)}, u32[]{:S(2)}, u32[]{:S(2)}) async-start(bf16[8,8,512]{2,1,0:T(8,128)(2,1)} %get-tuple-element.28.order_ref), calls=%async_computation.1 | async-start | bytes 131072 | tf_op jit(solution)/shard_map/all_to_all | solution.py:212
  25.1 23.5 %all-to-all-start.2 = ((bf16[64,8,128]{2,1,0:T(8,128)(2,1)}), bf16[64,8,128]{2,1,0:T(8,128)(2,1)S(1)}, u32[]{:S(2)}, u32[]{:S(2)}) async-start(bf16[64,8,128]{2,1,0:T(8,128)(2,1)} %get-tuple-element.30), calls=%async_computation.2 | async-start | bytes 262144 | tf_op jit(solution)/shard_map/all_to_all | solution.py:224
  36.7 7.9 %collective-permute-start = (bf16[8,8,512]{2,1,0:T(8,128)(2,1)S(1)}, bf16[8,8,512]{2,1,0:T(8,128)(2,1)S(1)}, u32[]{:S(2)}, u32[]{:S(2)}) collective-permute-start(bf16[8,8,512]{2,1,0:T(8,128)(2,1)S(1)} %all-to-all-done.1.b0), channel_id=1, source_target_pairs={{0,3},{1,2},{2,1},{3,0},{64,66},{65,67},{66,64},{67,65},{128,131},... | collective-permute-start | bytes 196616 | tf_op jit(solution)/shard_map/ppermute | solution.py:228
  40.7 8.6 %collective-permute-start.1 = (bf16[8,8,512]{2,1,0:T(8,128)(2,1)S(1)}, bf16[8,8,512]{2,1,0:T(8,128)(2,1)S(1)}, u32[]{:S(2)}, u32[]{:S(2)}) collective-permute-start(bf16[8,8,512]{2,1,0:T(8,128)(2,1)S(1)} %all-to-all-done.1.b0), channel_id=1, source_target_pairs={{0,1},{1,0},{2,3},{3,2},{4,5},{5,4},{6,7},{7,6},{8,9},{9,8},{10,11... | collective-permute-start | bytes 196616 | tf_op jit(solution)/shard_map/ppermute | solution.py:229
  44.6 4.9 %collective-permute-start.2 = (bf16[8,8,512]{2,1,0:T(8,128)(2,1)S(1)}, bf16[8,8,512]{2,1,0:T(8,128)(2,1)S(1)}, u32[]{:S(2)}, u32[]{:S(2)}) collective-permute-start(bf16[8,8,512]{2,1,0:T(8,128)(2,1)S(1)} %collective-permute-done.b1), channel_id=1, source_target_pairs={{0,64},{64,0},{128,192},{192,128},{256,320},{320,256},{384,448},{4... | collective-permute-start | bytes 196616 | tf_op jit(solution)/shard_map/ppermute | solution.py:230

commit v6 on v5

--- a/solution.py
+++ b/solution.py
@@ -96,7 +96,7 @@
         sb_ref[i] = block
 
 
-def prepare_kernel(ra_ref, codes_ref, scale_ref, left_ref, frozen_ref, asc, wide):
+def prepare_kernel(ra_ref, codes_ref, scale_ref, left_ref, frozen_ref, asc, part, wide):
     cut = 64 - PLANE_FIRST
     asc[0 : 8 * PLANE_FIRST] = ra_ref[cut:64].astype(jnp.float32).reshape(8 * PLANE_FIRST, 128)
     asc[8 * PLANE_FIRST : 512] = ra_ref[0:cut].astype(jnp.float32).reshape(8 * cut, 128)
@@ -106,10 +106,11 @@
     wide[...] = jnp.zeros((12, 256, 128), jnp.float32)
     for i in range(4):
         peer = lax.bitwise_xor(me, steps[i])
+        part[...] = asc[pl.ds(pl.multiple_of(128 * peer, 128), 128), :]
         for l in range(2):
             for j in range(3):
                 for k in range(2):
-                    rows = asc[pl.ds(128 * peer + 8 * k + 3 * l + j, 8, stride=16), :]
+                    rows = part[pl.ds(8 * k + 3 * l + j, 8, stride=16), :]
                     rows = adapter_scale * jnp.concatenate([rows[4:8], rows[0:4]], axis=0)
                     for h in range(2):
                         wide[6 * l + 3 * h + j, pl.ds(64 * i + 4 * l + 2 * h + k, 8, stride=8), :] = rows
@@ -233,7 +234,11 @@
         out_shape=[sds((12, 128, 256), bf16), sds((2, 384, 896), f32)],
         in_specs=vmem(3),
         out_specs=vmem(2),
-        scratch_shapes=[pltpu.VMEM((512, 128), f32), pltpu.VMEM((12, 256, 128), f32)],
+        scratch_shapes=[
+            pltpu.VMEM((512, 128), f32),
+            pltpu.VMEM((128, 128), f32),
+            pltpu.VMEM((12, 256, 128), f32),
+        ],
         compiler_params=SMALL,
         cost_estimate=pl.CostEstimate(flops=10**6, bytes_accessed=4000000, transcendentals=0),
         name="prepare",

time: 51.6 us -> 51.6 us (level)
  no operation moved by 1% of the time
where the time goes in v6:
time: 51.6 us; the launch traced here: 51.1 us
  starting transfers between devices  29.1 us (56%)
  blocking collectives  14 us (27%)
  Pallas kernels  4.68 us (9%)
  waiting for transfers between devices  1.59 us (3%)
  local copies, waits for them, and re-layouts  0.96 us (2%)
  between operations  0.79 us (2%)
    all_to_all x1, blocking collectives, shards(): lax.all_to_all(messages, 'dp', 0, 0, tiled=True, axis_index_groups=[DP_OR...  14 us
    all_to_all x1, starting transfers between devices, shards(): lax.all_to_all(send_a, ('roll', 'tp'), 0, 0, tiled=True, axis_index_group...  11.6 us
    all_to_all x1, starting transfers between devices, shards(): lax.all_to_all(send_b, 'dp', 0, 0, tiled=True, axis_index_groups=[DP_ORDER])  6.48 us
    ppermute x1, starting transfers between devices, shards(): all_b.append(lax.ppermute(all_b[0], ('dp', 'tp'), far))  3.99 us
    ppermute x1, starting transfers between devices, shards(): all_b.append(lax.ppermute(all_b[1], 'dp', [(d, d ^ 1) for d in range(8)]))  3.98 us
    ppermute x1, starting transfers between devices, shards(): all_b.append(lax.ppermute(all_b[0], 'tp', [(t, t ^ 1) for t in range(4)]))  3.09 us
    pallas_call x1, Pallas kernels, shards(): pl.pallas_call(merge_kernel, out_shape=[sds((2, 384, 896), bf16), sds((3,...  1.65 us
    pallas_call x1, Pallas kernels, shards(): pl.pallas_call(adam_a_kernel, out_shape=a_state + [sds((64, 8, 128), bf16...  1.56 us
  transfers between devices with their start and end apart: 5, of which 3 were waited for; matrix products, arithmetic and copies ran while one was open for 0% of the time, Pallas kernels for 4%

profile of v6, /device:TPU:1, one launch (start us, length us, event | category | flops | bytes accessed | tf_op | source)
XLA Modules:
  0.0 51.1 jit_solution(10129541725199507493)
XLA Ops:
  0.6 0.0 copy-start.8
  0.6 0.0 copy-start.9
  0.7 0.9 %copy-done.8 = f32[1,2,16,896]{3,2,1,0:T(8,128)S(1)} copy-done((f32[1,2,16,896]{3,2,1,0:T(8,128)S(1)}, f32[1,2,16,896]{3,2,1,0:T(8,128)}, u32[]{:S(2)}) %copy-start.8) | copy-done | bytes 114712
  1.5 0.1 copy-done.9
  1.6 0.0 copy-start.1
  1.6 0.0 copy-start.2
  1.6 0.0 copy-start.3
  1.6 0.0 copy-start.4
  1.6 0.0 copy-start.5
  1.6 0.0 copy-start.6
  1.6 0.0 copy-start
  1.6 0.0 copy-start.7
  1.6 0.1 pack.1
  1.7 14.0 %all_to_all.15.r_ref = bf16[8,8,896]{2,1,0:T(8,128)(2,1)S(1)} all-to-all(bf16[8,8,896]{2,1,0:T(8,128)(2,1)S(1)} %pack.1), channel_id=1, replica_groups={{256,320,384,448,0,64,128,192},{257,321,385,449,1,65,129,193},{258,322,..., dimensions={0} | all-to-all | bytes 229376 | tf_op jit(solution)/shard_map/all_to_all | solution.py:200
  15.7 0.0 copy-done.1
  15.7 0.0 copy-done.2
  15.8 0.0 copy-done.3
  15.8 0.7 %adam_b.1 = (f32[2,2,896]{2,1,0:T(2,128)S(1)}, f32[2,2,896]{2,1,0:T(2,128)S(1)}, f32[2,2,896]{2,1,0:T(2,128)S(1)}, bf16[8,8,512]{2,1,0:T(8,128)(2,1)}) custom-call(bf16[8,8,896]{2,1,0:T(8,128)(2,1)S(1)} %all_to_all.15.r_ref, f32[2,2,896]{2,1,0:T(2,128)S(1)} %copy-done.1, f32[2,2,896]{2,1,0:T(2,128)S(1)} %copy-done.2, f32[2,2,896]{2,1,0:T(2,128)S(1)} %copy-done.3), custom_call_target="tpu_custom_call" | custom-call | flops 100000 | bytes 400000 | tf_op jit(solution)/shard_map/adam_b/pallas_call | solution.py:203
  16.4 6.5 %all-to-all-start.1 = ((bf16[8,8,512]{2,1,0:T(8,128)(2,1)}), bf16[8,8,512]{2,1,0:T(8,128)(2,1)S(1)}, u32[]{:S(2)}, u32[]{:S(2)}) async-start(bf16[8,8,512]{2,1,0:T(8,128)(2,1)} %get-tuple-element.28.order_ref), calls=%async_computation.1 | async-start | bytes 131072 | tf_op jit(solution)/shard_map/all_to_all | solution.py:213
  22.9 0.0 copy-done.4
  22.9 0.0 copy-done.5
  22.9 0.0 copy-done.6
  22.9 1.6 %adam_a.1 = (f32[24,128]{1,0:T(8,128)S(1)}, f32[24,128]{1,0:T(8,128)S(1)}, f32[24,128]{1,0:T(8,128)S(1)}, bf16[64,8,128]{2,1,0:T(8,128)(2,1)}) custom-call(bf16[8,8,896]{2,1,0:T(8,128)(2,1)S(1)} %all_to_all.15.r_ref, f32[24,128]{1,0:T(8,128)S(1)} %bitcast.9, f32[24,128]{1,0:T(8,128)S(1)} %bitcast.10, f32[24,128]{1,0:T(8,128)S(1)} %bitcast.11, ...), custom_call_target="tpu_custom_call" | custom-call | flops 100000 | bytes 200000 | tf_op jit(solution)/shard_map/adam_a/pallas_call | solution.py:214
  24.5 0.6 %all-to-all-done.1.b0 = bf16[8,8,512]{2,1,0:T(8,128)(2,1)S(1)} async-done(((bf16[8,8,512]{2,1,0:T(8,128)(2,1)}), bf16[8,8,512]{2,1,0:T(8,128)(2,1)S(1)}, u32[]{:S(2)}, u32[]{:S(2)}) %all-to-all-start.1) | async-done | bytes 65568 | tf_op jit(solution)/shard_map/all_to_all | solution.py:213
  25.1 11.6 %all-to-all-start.2 = ((bf16[64,8,128]{2,1,0:T(8,128)(2,1)}), bf16[64,8,128]{2,1,0:T(8,128)(2,1)S(1)}, u32[]{:S(2)}, u32[]{:S(2)}) async-start(bf16[64,8,128]{2,1,0:T(8,128)(2,1)} %get-tuple-element.30), calls=%async_computation.2 | async-start | bytes 262144 | tf_op jit(solution)/shard_map/all_to_all | solution.py:225
  36.7 4.0 %collective-permute-start = (bf16[8,8,512]{2,1,0:T(8,128)(2,1)S(1)}, bf16[8,8,512]{2,1,0:T(8,128)(2,1)S(1)}, u32[]{:S(2)}, u32[]{:S(2)}) collective-permute-start(bf16[8,8,512]{2,1,0:T(8,128)(2,1)S(1)} %all-to-all-done.1.b0), channel_id=1, source_target_pairs={{0,3},{1,2},{2,1},{3,0},{64,66},{65,67},{66,64},{67,65},{128,131},... | collective-permute-start | bytes 196616 | tf_op jit(solution)/shard_map/ppermute | solution.py:229
  40.7 3.1 %collective-permute-start.1 = (bf16[8,8,512]{2,1,0:T(8,128)(2,1)S(1)}, bf16[8,8,512]{2,1,0:T(8,128)(2,1)S(1)}, u32[]{:S(2)}, u32[]{:S(2)}) collective-permute-start(bf16[8,8,512]{2,1,0:T(8,128)(2,1)S(1)} %all-to-all-done.1.b0), channel_id=1, source_target_pairs={{0,1},{1,0},{2,3},{3,2},{4,5},{5,4},{6,7},{7,6},{8,9},{9,8},{10,11... | collective-permute-start | bytes 196616 | tf_op jit(solution)/shard_map/ppermute | solution.py:230
  43.8 0.8 %collective-permute-done.b1 = bf16[8,8,512]{2,1,0:T(8,128)(2,1)S(1)} collective-permute-done((bf16[8,8,512]{2,1,0:T(8,128)(2,1)S(1)}, bf16[8,8,512]{2,1,0:T(8,128)(2,1)S(1)}, u32[]{:S(2)}, u32[]{:S(2)}) %collective-permute-start) | collective-permute-done | bytes 65568 | tf_op jit(solution)/shard_map/ppermute | solution.py:229
  44.6 4.0 %collective-permute-start.2 = (bf16[8,8,512]{2,1,0:T(8,128)(2,1)S(1)}, bf16[8,8,512]{2,1,0:T(8,128)(2,1)S(1)}, u32[]{:S(2)}, u32[]{:S(2)}) collective-permute-start(bf16[8,8,512]{2,1,0:T(8,128)(2,1)S(1)} %collective-permute-done.b1), channel_id=1, source_target_pairs={{0,64},{64,0},{128,192},{192,128},{256,320},{320,256},{384,448},{4... | collective-permute-start | bytes 196616 | tf_op jit(solution)/shard_map/ppermute | solution.py:231
  48.6 0.0 all-to-all-done.2.ra_ref
  48.6 0.0 copy-done
  48.6 0.0 copy-done.7
  48.6 0.7 %prepare.1 = (bf16[12,128,256]{2,1,0:T(8,128)(2,1)S(1)}, f32[2,384,896]{2,1,0:T(8,128)S(1)}) custom-call(bf16[64,8,128]{2,1,0:T(8,128)(2,1)S(1)} %all-to-all-done.2.ra_ref, bf16[2,384,896]{2,1,0:T(8,128)(2,1)S(1)} %copy-done, f32[3,2,7]{2,1,0:T(2,128)S(1)} %bitcast.12), custom_call_target="tpu_custom_call" | custom-call | flops 1000000 | bytes 4000000 | tf_op jit(solution)/shard_map/prepare/pallas_call | solution.py:232
  49.4 0.0 collective-permute-done.1.b2
  49.4 0.1 collective-permute-done.2.b3
  49.5 1.6 %merge.1 = (bf16[2,384,896]{2,1,0:T(8,128)(2,1)}, f32[3,2,7]{2,1,0:T(2,128)}, f32[24,128]{1,0:T(8,128)}, f32[24,128]{1,0:T(8,128)}, f32[24,128]{1,0:T(8,128)}, /...) custom-call(bf16[12,128,256]{2,1,0:T(8,128)(2,1)S(1)} %get-tuple-element.31.left_ref, ...), custom_call_target="tpu_custom_call" | custom-call | tf_op jit(solution)/shard_map/merge/pallas_call | solution.py:246
  (1 shorter events, 0.0 us)
Async XLA Ops:
  0.6 0.9 %copy-start.8 = (f32[1,2,16,896]{3,2,1,0:T(8,128)S(1)}, f32[1,2,16,896]{3,2,1,0:T(8,128)}, u32[]{:S(2)}) copy-start(f32[1,2,16,896]{3,2,1,0:T(8,128)} %gb_ref.1) | copy-start | bytes 344068
  0.6 0.9 %copy-start.9 = (f32[1,2,1,12288]{3,2,1,0:T(1,128)S(1)}, f32[1,2,1,12288]{3,2,1,0:T(1,128)}, u32[]{:S(2)}) copy-start(f32[1,2,1,12288]{3,2,1,0:T(1,128)} %param.10) | copy-start | bytes 294916
  1.6 14.2 %copy-start.1 = (f32[2,2,896]{2,1,0:T(2,128)S(1)}, f32[2,2,896]{2,1,0:T(2,128)}, u32[]{:S(2)}) copy-start(f32[2,2,896]{2,1,0:T(2,128)} %pb.1) | copy-start | bytes 43012
  1.6 14.2 %copy-start.2 = (f32[2,2,896]{2,1,0:T(2,128)S(1)}, f32[2,2,896]{2,1,0:T(2,128)}, u32[]{:S(2)}) copy-start(f32[2,2,896]{2,1,0:T(2,128)} %mb.1) | copy-start | bytes 43012
  1.6 14.2 %copy-start.3 = (f32[2,2,896]{2,1,0:T(2,128)S(1)}, f32[2,2,896]{2,1,0:T(2,128)}, u32[]{:S(2)}) copy-start(f32[2,2,896]{2,1,0:T(2,128)} %vb.1) | copy-start | bytes 43012
  1.6 21.3 %copy-start.4 = (f32[2,1,1536]{2,1,0:T(1,128)S(1)}, f32[2,1,1536]{2,1,0:T(1,128)}, u32[]{:S(2)}) copy-start(f32[2,1,1536]{2,1,0:T(1,128)} %param.12) | copy-start | bytes 36868
  1.6 21.3 %copy-start.5 = (f32[2,1,1536]{2,1,0:T(1,128)S(1)}, f32[2,1,1536]{2,1,0:T(1,128)}, u32[]{:S(2)}) copy-start(f32[2,1,1536]{2,1,0:T(1,128)} %param.13) | copy-start | bytes 36868
  1.6 21.3 %copy-start.6 = (f32[2,1,1536]{2,1,0:T(1,128)S(1)}, f32[2,1,1536]{2,1,0:T(1,128)}, u32[]{:S(2)}) copy-start(f32[2,1,1536]{2,1,0:T(1,128)} %param.14) | copy-start | bytes 36868
  1.6 47.0 %copy-start = (bf16[2,384,896]{2,1,0:T(8,128)(2,1)S(1)}, bf16[2,384,896]{2,1,0:T(8,128)(2,1)}, u32[]{:S(2)}) copy-start(bf16[2,384,896]{2,1,0:T(8,128)(2,1)} %codes_ref.1) | copy-start | bytes 4128772
  1.6 47.0 %copy-start.7 = (f32[2,3,7]{2,0,1:T(2,128)S(1)}, f32[2,3,7]{2,0,1:T(2,128)}, u32[]{:S(2)}) copy-start(f32[2,3,7]{2,0,1:T(2,128)} %param.19) | copy-start | bytes 508
  16.4 8.7 %all-to-all-start.1 = ((bf16[8,8,512]{2,1,0:T(8,128)(2,1)}), bf16[8,8,512]{2,1,0:T(8,128)(2,1)S(1)}, u32[]{:S(2)}, u32[]{:S(2)}) async-start(bf16[8,8,512]{2,1,0:T(8,128)(2,1)} %get-tuple-element.28.order_ref), calls=%async_computation.1 | async-start | bytes 131072 | tf_op jit(solution)/shard_map/all_to_all | solution.py:213
  25.1 23.5 %all-to-all-start.2 = ((bf16[64,8,128]{2,1,0:T(8,128)(2,1)}), bf16[64,8,128]{2,1,0:T(8,128)(2,1)S(1)}, u32[]{:S(2)}, u32[]{:S(2)}) async-start(bf16[64,8,128]{2,1,0:T(8,128)(2,1)} %get-tuple-element.30), calls=%async_computation.2 | async-start | bytes 262144 | tf_op jit(solution)/shard_map/all_to_all | solution.py:225
  36.7 7.9 %collective-permute-start = (bf16[8,8,512]{2,1,0:T(8,128)(2,1)S(1)}, bf16[8,8,512]{2,1,0:T(8,128)(2,1)S(1)}, u32[]{:S(2)}, u32[]{:S(2)}) collective-permute-start(bf16[8,8,512]{2,1,0:T(8,128)(2,1)S(1)} %all-to-all-done.1.b0), channel_id=1, source_target_pairs={{0,3},{1,2},{2,1},{3,0},{64,66},{65,67},{66,64},{67,65},{128,131},... | collective-permute-start | bytes 196616 | tf_op jit(solution)/shard_map/ppermute | solution.py:229
  40.7 8.7 %collective-permute-start.1 = (bf16[8,8,512]{2,1,0:T(8,128)(2,1)S(1)}, bf16[8,8,512]{2,1,0:T(8,128)(2,1)S(1)}, u32[]{:S(2)}, u32[]{:S(2)}) collective-permute-start(bf16[8,8,512]{2,1,0:T(8,128)(2,1)S(1)} %all-to-all-done.1.b0), channel_id=1, source_target_pairs={{0,1},{1,0},{2,3},{3,2},{4,5},{5,4},{6,7},{7,6},{8,9},{9,8},{10,11... | collective-permute-start | bytes 196616 | tf_op jit(solution)/shard_map/ppermute | solution.py:230
  44.6 4.9 %collective-permute-start.2 = (bf16[8,8,512]{2,1,0:T(8,128)(2,1)S(1)}, bf16[8,8,512]{2,1,0:T(8,128)(2,1)S(1)}, u32[]{:S(2)}, u32[]{:S(2)}) collective-permute-start(bf16[8,8,512]{2,1,0:T(8,128)(2,1)S(1)} %collective-permute-done.b1), channel_id=1, source_target_pairs={{0,64},{64,0},{128,192},{192,128},{256,320},{320,256},{384,448},{4... | collective-permute-start | bytes 196616 | tf_op jit(solution)/shard_map/ppermute | solution.py:231

commit v7 on v6

--- a/solution.py
+++ b/solution.py
@@ -102,7 +102,7 @@
     asc[8 * PLANE_FIRST : 512] = ra_ref[0:cut].astype(jnp.float32).reshape(8 * cut, 128)
     me = lax.axis_index("tp")
     core = lax.rem(lax.axis_index("dp"), 2)
-    steps = (0, 3 - core, 1, 2 + core)
+    steps = (0, 2 + core, 1, 3 - core)
     wide[...] = jnp.zeros((12, 256, 128), jnp.float32)
     for i in range(4):
         peer = lax.bitwise_xor(me, steps[i])
@@ -225,7 +225,7 @@
     all_a = lax.all_to_all(
         send_a, ("roll", "tp"), 0, 0, tiled=True, axis_index_groups=[PLANE_ORDER]
     )
-    far = [(4 * d + t, 4 * d + (t ^ (3 - d % 2))) for d in range(8) for t in range(4)]
+    far = [(4 * d + t, 4 * d + (t ^ (2 + d % 2))) for d in range(8) for t in range(4)]
     all_b.append(lax.ppermute(all_b[0], ("dp", "tp"), far))
     all_b.append(lax.ppermute(all_b[0], "tp", [(t, t ^ 1) for t in range(4)]))
     all_b.append(lax.ppermute(all_b[1], "dp", [(d, d ^ 1) for d in range(8)]))

time: 51.6 us -> 51.3 us (level)
    ppermute x1, starting transfers between devices: 3.09 us -> 1.92 us  [shards(): all_b.append(lax.ppermute(all_b[0], 'tp', [(t, t ^ 1) for t in range(4)]))]
    ppermute x1, starting transfers between devices: 3.99 us -> 4.89 us  [shards(): all_b.append(lax.ppermute(all_b[0], ('dp', 'tp'), far))]
where the time goes in v7:
time: 51.3 us; the launch traced here: 50.9 us
  starting transfers between devices  28.7 us (56%)
  blocking collectives  14 us (27%)
  Pallas kernels  4.68 us (9%)
  waiting for transfers between devices  1.69 us (3%)
  local copies, waits for them, and re-layouts  0.96 us (2%)
  between operations  0.79 us (2%)
    all_to_all x1, blocking collectives, shards(): lax.all_to_all(messages, 'dp', 0, 0, tiled=True, axis_index_groups=[DP_OR...  14 us
    all_to_all x1, starting transfers between devices, shards(): lax.all_to_all(send_a, ('roll', 'tp'), 0, 0, tiled=True, axis_index_group...  11.6 us
    all_to_all x1, starting transfers between devices, shards(): lax.all_to_all(send_b, 'dp', 0, 0, tiled=True, axis_index_groups=[DP_ORDER])  6.48 us
    ppermute x1, starting transfers between devices, shards(): all_b.append(lax.ppermute(all_b[0], ('dp', 'tp'), far))  4.89 us
    ppermute x1, starting transfers between devices, shards(): all_b.append(lax.ppermute(all_b[1], 'dp', [(d, d ^ 1) for d in range(8)]))  3.88 us
    ppermute x1, starting transfers between devices, shards(): all_b.append(lax.ppermute(all_b[0], 'tp', [(t, t ^ 1) for t in range(4)]))  1.92 us
    pallas_call x1, Pallas kernels, shards(): pl.pallas_call(merge_kernel, out_shape=[sds((2, 384, 896), bf16), sds((3,...  1.64 us
    pallas_call x1, Pallas kernels, shards(): pl.pallas_call(adam_a_kernel, out_shape=a_state + [sds((64, 8, 128), bf16...  1.56 us
  transfers between devices with their start and end apart: 5, of which 3 were waited for; matrix products, arithmetic and copies ran while one was open for 0% of the time, Pallas kernels for 4%

profile of v7, /device:TPU:1, one launch (start us, length us, event | category | flops | bytes accessed | tf_op | source)
XLA Modules:
  0.0 50.9 jit_solution(12620010877401827423)
XLA Ops:
  0.6 0.0 copy-start.8
  0.6 0.0 copy-start.9
  0.7 0.9 %copy-done.8 = f32[1,2,16,896]{3,2,1,0:T(8,128)S(1)} copy-done((f32[1,2,16,896]{3,2,1,0:T(8,128)S(1)}, f32[1,2,16,896]{3,2,1,0:T(8,128)}, u32[]{:S(2)}) %copy-start.8) | copy-done | bytes 114712
  1.5 0.1 copy-done.9
  1.6 0.0 copy-start.1
  1.6 0.0 copy-start.2
  1.6 0.0 copy-start.3
  1.6 0.0 copy-start.4
  1.6 0.0 copy-start.5
  1.6 0.0 copy-start.6
  1.6 0.0 copy-start
  1.6 0.0 copy-start.7
  1.6 0.1 pack.1
  1.7 14.0 %all_to_all.15.r_ref = bf16[8,8,896]{2,1,0:T(8,128)(2,1)S(1)} all-to-all(bf16[8,8,896]{2,1,0:T(8,128)(2,1)S(1)} %pack.1), channel_id=1, replica_groups={{256,320,384,448,0,64,128,192},{257,321,385,449,1,65,129,193},{258,322,..., dimensions={0} | all-to-all | bytes 229376 | tf_op jit(solution)/shard_map/all_to_all | solution.py:200
  15.7 0.0 copy-done.1
  15.7 0.0 copy-done.2
  15.8 0.0 copy-done.3
  15.8 0.7 %adam_b.1 = (f32[2,2,896]{2,1,0:T(2,128)S(1)}, f32[2,2,896]{2,1,0:T(2,128)S(1)}, f32[2,2,896]{2,1,0:T(2,128)S(1)}, bf16[8,8,512]{2,1,0:T(8,128)(2,1)}) custom-call(bf16[8,8,896]{2,1,0:T(8,128)(2,1)S(1)} %all_to_all.15.r_ref, f32[2,2,896]{2,1,0:T(2,128)S(1)} %copy-done.1, f32[2,2,896]{2,1,0:T(2,128)S(1)} %copy-done.2, f32[2,2,896]{2,1,0:T(2,128)S(1)} %copy-done.3), custom_call_target="tpu_custom_call" | custom-call | flops 100000 | bytes 400000 | tf_op jit(solution)/shard_map/adam_b/pallas_call | solution.py:203
  16.4 6.5 %all-to-all-start.1 = ((bf16[8,8,512]{2,1,0:T(8,128)(2,1)}), bf16[8,8,512]{2,1,0:T(8,128)(2,1)S(1)}, u32[]{:S(2)}, u32[]{:S(2)}) async-start(bf16[8,8,512]{2,1,0:T(8,128)(2,1)} %get-tuple-element.28.order_ref), calls=%async_computation.1 | async-start | bytes 131072 | tf_op jit(solution)/shard_map/all_to_all | solution.py:213
  22.9 0.0 copy-done.4
  22.9 0.0 copy-done.5
  22.9 0.0 copy-done.6
  22.9 1.6 %adam_a.1 = (f32[24,128]{1,0:T(8,128)S(1)}, f32[24,128]{1,0:T(8,128)S(1)}, f32[24,128]{1,0:T(8,128)S(1)}, bf16[64,8,128]{2,1,0:T(8,128)(2,1)}) custom-call(bf16[8,8,896]{2,1,0:T(8,128)(2,1)S(1)} %all_to_all.15.r_ref, f32[24,128]{1,0:T(8,128)S(1)} %bitcast.9, f32[24,128]{1,0:T(8,128)S(1)} %bitcast.10, f32[24,128]{1,0:T(8,128)S(1)} %bitcast.11, ...), custom_call_target="tpu_custom_call" | custom-call | flops 100000 | bytes 200000 | tf_op jit(solution)/shard_map/adam_a/pallas_call | solution.py:214
  24.5 0.6 %all-to-all-done.1.b0 = bf16[8,8,512]{2,1,0:T(8,128)(2,1)S(1)} async-done(((bf16[8,8,512]{2,1,0:T(8,128)(2,1)}), bf16[8,8,512]{2,1,0:T(8,128)(2,1)S(1)}, u32[]{:S(2)}, u32[]{:S(2)}) %all-to-all-start.1) | async-done | bytes 65568 | tf_op jit(solution)/shard_map/all_to_all | solution.py:213
  25.1 11.6 %all-to-all-start.2 = ((bf16[64,8,128]{2,1,0:T(8,128)(2,1)}), bf16[64,8,128]{2,1,0:T(8,128)(2,1)S(1)}, u32[]{:S(2)}, u32[]{:S(2)}) async-start(bf16[64,8,128]{2,1,0:T(8,128)(2,1)} %get-tuple-element.30), calls=%async_computation.2 | async-start | bytes 262144 | tf_op jit(solution)/shard_map/all_to_all | solution.py:225
  36.7 4.9 %collective-permute-start = (bf16[8,8,512]{2,1,0:T(8,128)(2,1)S(1)}, bf16[8,8,512]{2,1,0:T(8,128)(2,1)S(1)}, u32[]{:S(2)}, u32[]{:S(2)}) collective-permute-start(bf16[8,8,512]{2,1,0:T(8,128)(2,1)S(1)} %all-to-all-done.1.b0), channel_id=1, source_target_pairs={{0,2},{1,3},{2,0},{3,1},{64,67},{65,66},{66,65},{67,64},{128,130},... | collective-permute-start | bytes 196616 | tf_op jit(solution)/shard_map/ppermute | solution.py:229
  41.6 1.9 %collective-permute-start.1 = (bf16[8,8,512]{2,1,0:T(8,128)(2,1)S(1)}, bf16[8,8,512]{2,1,0:T(8,128)(2,1)S(1)}, u32[]{:S(2)}, u32[]{:S(2)}) collective-permute-start(bf16[8,8,512]{2,1,0:T(8,128)(2,1)S(1)} %all-to-all-done.1.b0), channel_id=1, source_target_pairs={{0,1},{1,0},{2,3},{3,2},{4,5},{5,4},{6,7},{7,6},{8,9},{9,8},{10,11... | collective-permute-start | bytes 196616 | tf_op jit(solution)/shard_map/ppermute | solution.py:230
  43.5 0.9 %collective-permute-done.b1 = bf16[8,8,512]{2,1,0:T(8,128)(2,1)S(1)} collective-permute-done((bf16[8,8,512]{2,1,0:T(8,128)(2,1)S(1)}, bf16[8,8,512]{2,1,0:T(8,128)(2,1)S(1)}, u32[]{:S(2)}, u32[]{:S(2)}) %collective-permute-start) | collective-permute-done | bytes 65568 | tf_op jit(solution)/shard_map/ppermute | solution.py:229
  44.5 3.9 %collective-permute-start.2 = (bf16[8,8,512]{2,1,0:T(8,128)(2,1)S(1)}, bf16[8,8,512]{2,1,0:T(8,128)(2,1)S(1)}, u32[]{:S(2)}, u32[]{:S(2)}) collective-permute-start(bf16[8,8,512]{2,1,0:T(8,128)(2,1)S(1)} %collective-permute-done.b1), channel_id=1, source_target_pairs={{0,64},{64,0},{128,192},{192,128},{256,320},{320,256},{384,448},{4... | collective-permute-start | bytes 196616 | tf_op jit(solution)/shard_map/ppermute | solution.py:231
  48.3 0.0 all-to-all-done.2.ra_ref
  48.3 0.0 copy-done
  48.4 0.0 copy-done.7
  48.4 0.7 %prepare.1 = (bf16[12,128,256]{2,1,0:T(8,128)(2,1)S(1)}, f32[2,384,896]{2,1,0:T(8,128)S(1)}) custom-call(bf16[64,8,128]{2,1,0:T(8,128)(2,1)S(1)} %all-to-all-done.2.ra_ref, bf16[2,384,896]{2,1,0:T(8,128)(2,1)S(1)} %copy-done, f32[3,2,7]{2,1,0:T(2,128)S(1)} %bitcast.12), custom_call_target="tpu_custom_call" | custom-call | flops 1000000 | bytes 4000000 | tf_op jit(solution)/shard_map/prepare/pallas_call | solution.py:232
  49.1 0.0 collective-permute-done.1.b2
  49.1 0.1 collective-permute-done.2.b3
  49.2 1.6 %merge.1 = (bf16[2,384,896]{2,1,0:T(8,128)(2,1)}, f32[3,2,7]{2,1,0:T(2,128)}, f32[24,128]{1,0:T(8,128)}, f32[24,128]{1,0:T(8,128)}, f32[24,128]{1,0:T(8,128)}, /...) custom-call(bf16[12,128,256]{2,1,0:T(8,128)(2,1)S(1)} %get-tuple-element.31.left_ref, ...), custom_call_target="tpu_custom_call" | custom-call | tf_op jit(solution)/shard_map/merge/pallas_call | solution.py:246
  (1 shorter events, 0.0 us)
Async XLA Ops:
  0.6 0.9 %copy-start.8 = (f32[1,2,16,896]{3,2,1,0:T(8,128)S(1)}, f32[1,2,16,896]{3,2,1,0:T(8,128)}, u32[]{:S(2)}) copy-start(f32[1,2,16,896]{3,2,1,0:T(8,128)} %gb_ref.1) | copy-start | bytes 344068
  0.6 0.9 %copy-start.9 = (f32[1,2,1,12288]{3,2,1,0:T(1,128)S(1)}, f32[1,2,1,12288]{3,2,1,0:T(1,128)}, u32[]{:S(2)}) copy-start(f32[1,2,1,12288]{3,2,1,0:T(1,128)} %param.10) | copy-start | bytes 294916
  1.6 14.2 %copy-start.1 = (f32[2,2,896]{2,1,0:T(2,128)S(1)}, f32[2,2,896]{2,1,0:T(2,128)}, u32[]{:S(2)}) copy-start(f32[2,2,896]{2,1,0:T(2,128)} %pb.1) | copy-start | bytes 43012
  1.6 14.2 %copy-start.2 = (f32[2,2,896]{2,1,0:T(2,128)S(1)}, f32[2,2,896]{2,1,0:T(2,128)}, u32[]{:S(2)}) copy-start(f32[2,2,896]{2,1,0:T(2,128)} %mb.1) | copy-start | bytes 43012
  1.6 14.2 %copy-start.3 = (f32[2,2,896]{2,1,0:T(2,128)S(1)}, f32[2,2,896]{2,1,0:T(2,128)}, u32[]{:S(2)}) copy-start(f32[2,2,896]{2,1,0:T(2,128)} %vb.1) | copy-start | bytes 43012
  1.6 21.3 %copy-start.4 = (f32[2,1,1536]{2,1,0:T(1,128)S(1)}, f32[2,1,1536]{2,1,0:T(1,128)}, u32[]{:S(2)}) copy-start(f32[2,1,1536]{2,1,0:T(1,128)} %param.12) | copy-start | bytes 36868
  1.6 21.3 %copy-start.5 = (f32[2,1,1536]{2,1,0:T(1,128)S(1)}, f32[2,1,1536]{2,1,0:T(1,128)}, u32[]{:S(2)}) copy-start(f32[2,1,1536]{2,1,0:T(1,128)} %param.13) | copy-start | bytes 36868
  1.6 21.3 %copy-start.6 = (f32[2,1,1536]{2,1,0:T(1,128)S(1)}, f32[2,1,1536]{2,1,0:T(1,128)}, u32[]{:S(2)}) copy-start(f32[2,1,1536]{2,1,0:T(1,128)} %param.14) | copy-start | bytes 36868
  1.6 46.7 %copy-start = (bf16[2,384,896]{2,1,0:T(8,128)(2,1)S(1)}, bf16[2,384,896]{2,1,0:T(8,128)(2,1)}, u32[]{:S(2)}) copy-start(bf16[2,384,896]{2,1,0:T(8,128)(2,1)} %codes_ref.1) | copy-start | bytes 4128772
  1.6 46.7 %copy-start.7 = (f32[2,3,7]{2,0,1:T(2,128)S(1)}, f32[2,3,7]{2,0,1:T(2,128)}, u32[]{:S(2)}) copy-start(f32[2,3,7]{2,0,1:T(2,128)} %param.19) | copy-start | bytes 508
  16.4 8.7 %all-to-all-start.1 = ((bf16[8,8,512]{2,1,0:T(8,128)(2,1)}), bf16[8,8,512]{2,1,0:T(8,128)(2,1)S(1)}, u32[]{:S(2)}, u32[]{:S(2)}) async-start(bf16[8,8,512]{2,1,0:T(8,128)(2,1)} %get-tuple-element.28.order_ref), calls=%async_computation.1 | async-start | bytes 131072 | tf_op jit(solution)/shard_map/all_to_all | solution.py:213
  25.1 23.2 %all-to-all-start.2 = ((bf16[64,8,128]{2,1,0:T(8,128)(2,1)}), bf16[64,8,128]{2,1,0:T(8,128)(2,1)S(1)}, u32[]{:S(2)}, u32[]{:S(2)}) async-start(bf16[64,8,128]{2,1,0:T(8,128)(2,1)} %get-tuple-element.30), calls=%async_computation.2 | async-start | bytes 262144 | tf_op jit(solution)/shard_map/all_to_all | solution.py:225
  36.7 7.8 %collective-permute-start = (bf16[8,8,512]{2,1,0:T(8,128)(2,1)S(1)}, bf16[8,8,512]{2,1,0:T(8,128)(2,1)S(1)}, u32[]{:S(2)}, u32[]{:S(2)}) collective-permute-start(bf16[8,8,512]{2,1,0:T(8,128)(2,1)S(1)} %all-to-all-done.1.b0), channel_id=1, source_target_pairs={{0,2},{1,3},{2,0},{3,1},{64,67},{65,66},{66,65},{67,64},{128,130},... | collective-permute-start | bytes 196616 | tf_op jit(solution)/shard_map/ppermute | solution.py:229
  41.6 7.5 %collective-permute-start.1 = (bf16[8,8,512]{2,1,0:T(8,128)(2,1)S(1)}, bf16[8,8,512]{2,1,0:T(8,128)(2,1)S(1)}, u32[]{:S(2)}, u32[]{:S(2)}) collective-permute-start(bf16[8,8,512]{2,1,0:T(8,128)(2,1)S(1)} %all-to-all-done.1.b0), channel_id=1, source_target_pairs={{0,1},{1,0},{2,3},{3,2},{4,5},{5,4},{6,7},{7,6},{8,9},{9,8},{10,11... | collective-permute-start | bytes 196616 | tf_op jit(solution)/shard_map/ppermute | solution.py:230
  44.5 4.8 %collective-permute-start.2 = (bf16[8,8,512]{2,1,0:T(8,128)(2,1)S(1)}, bf16[8,8,512]{2,1,0:T(8,128)(2,1)S(1)}, u32[]{:S(2)}, u32[]{:S(2)}) collective-permute-start(bf16[8,8,512]{2,1,0:T(8,128)(2,1)S(1)} %collective-permute-done.b1), channel_id=1, source_target_pairs={{0,64},{64,0},{128,192},{192,128},{256,320},{320,256},{384,448},{4... | collective-permute-start | bytes 196616 | tf_op jit(solution)/shard_map/ppermute | solution.py:231
